TPU v7x, 32 devices: a whole 2x2x4 slice. The times are simulated.
32 devices in a mesh: var: 2 (over y), gx: 4 (over z), gy: 2 (over x), nd: 2 (over core).
Axes of the slice: x: 2, y: 2, z: 4, core: 2. Of those that a mesh axis runs over, the one named last changes fastest.
Arguments:
- right_side: float32 [8192, 256], P(('var', 'gx', 'gy', 'nd')), parts along dimension 0, may hold values from -8 to 8
- node_diag: float32 [8192], P(('var', 'gx', 'gy', 'nd')), parts along dimension 0, may hold values from 1 to 10
- local_coup: float32 [64, 7, 128, 128], P(('var', 'gx', 'gy', 'nd')), parts along dimension 0, may hold values from -0.01 to 0.01
- block_cols: int32 [32, 7], P(('gx', 'gy', 'nd')), may hold values from 0 to 3
- border_coup: float32 [32, 8, 128, 128], P(('var', 'gx', 'gy', 'nd')), parts along dimension 0, may hold values from -0.01 to 0.01
- border_send: int32 [16, 8], P(('gx', 'gy', 'nd')), may hold values from 0 to 1
- border_rows: int32 [16, 8], P(('gx', 'gy', 'nd')), may hold values from 0 to 1
Outputs:
- solution_field: float32 [8192, 256], P(('var', 'gx', 'gy', 'nd')), parts along dimension 0
There are 2 independent parts, one for each index of `var`. A program takes and returns all parts, laid end to end along the dimension named above; an argument that names none is the same for every part. Nothing has to cross between parts.
Inputs may be any that keep to these rules, and one draw needn't show every extreme that they name: `block_cols`: block numbers within a patch. `border_send`: block numbers within the sending device. `border_rows`: block numbers within the receiving device.
All inputs are finite; a program needn't handle non-finite values.
Results may differ from a plain program's by a relative error of at most 0.0003.
Values sent between devices are 32-bit elements; how exact they have to be, the bound alone decides.
A program may use at most 64 MiB of HBM per device.

v0:
```python
import jax
import jax.numpy as jnp
from jax import lax
from jax.sharding import PartitionSpec as P

ITERS = 2


def with_halo(cells, sides, width, closed):
    for axis, dim in sides:
        count = lax.axis_size(axis)
        ends = count if closed else count - 1
        head = lax.slice_in_dim(cells, 0, width, axis=dim)
        tail = lax.slice_in_dim(cells, cells.shape[dim] - width, cells.shape[dim], axis=dim)
        cells = jnp.concatenate(
            [
                lax.ppermute(tail, axis, [(i, (i + 1) % count) for i in range(ends)]),
                cells,
                lax.ppermute(head, axis, [((i + 1) % count, i) for i in range(ends)]),
            ],
            axis=dim,
        )
    return cells


def apply_prec(field, node_diag, local_coup, block_cols, border_coup, border_send, border_rows):
    hp = lax.Precision.HIGHEST
    nblocks = local_coup.shape[0]
    nonzeros = local_coup.shape[1]
    bsize = local_coup.shape[2]
    width = field.shape[1]
    blocks = field.reshape(nblocks, bsize, width)
    patch = lax.all_gather(blocks, "nd", axis=0, tiled=True)
    picked = jnp.take(patch, block_cols, axis=0)
    result = node_diag.reshape(nblocks, bsize, 1) * blocks
    result = result + jnp.einsum("bkij,bkjc->bic", local_coup, picked, precision=hp)
    patch_len = patch.shape[0]
    tterms = jnp.einsum("bkji,bjc->bkic", local_coup, blocks, precision=hp).reshape(
        nblocks * nonzeros, bsize, width
    )
    tonehot = (
        block_cols.reshape(nblocks * nonzeros)[None, :]
        == jnp.arange(patch_len, dtype=jnp.int32)[:, None]
    ).astype(jnp.float32)
    spread = jnp.einsum("pq,qic->pic", tonehot, tterms, precision=hp)
    result = result + lax.psum_scatter(spread, "nd", scatter_dimension=0, tiled=True)
    chosen = jnp.take(blocks, border_send[0], axis=0)
    per_side = chosen.shape[0] // 4
    slots = chosen.reshape(4, per_side, bsize, width)
    own_rows = jnp.take(blocks, border_rows[0], axis=0)
    back = jnp.einsum("mji,mjc->mic", border_coup[0], own_rows, precision=hp)
    back_sides = back.reshape(4, per_side, bsize, width)
    along = with_halo(jnp.stack([slots[1], slots[0]]), (("gx", 0),), 1, True)
    across = with_halo(jnp.stack([slots[3], slots[2]]), (("gy", 0),), 1, False)
    received = jnp.concatenate([along[0], along[3], across[0], across[3]], axis=0)
    back_x = with_halo(jnp.stack([back_sides[0], back_sides[1]]), (("gx", 0),), 1, True)
    back_y = with_halo(jnp.stack([back_sides[2], back_sides[3]]), (("gy", 0),), 1, False)
    returned = jnp.concatenate([back_x[3], back_x[0], back_y[3], back_y[0]], axis=0)
    contrib = jnp.einsum("mij,mjc->mic", border_coup[0], received, precision=hp)
    onehot = (border_rows[0][None, :] == jnp.arange(nblocks, dtype=jnp.int32)[:, None]).astype(
        jnp.float32
    )
    result = result + jnp.einsum("nm,mic->nic", onehot, contrib, precision=hp)
    sonehot = (border_send[0][None, :] == jnp.arange(nblocks, dtype=jnp.int32)[:, None]).astype(
        jnp.float32
    )
    result = result + jnp.einsum("nm,mic->nic", sonehot, returned, precision=hp)
    return result.reshape(nblocks * bsize, width)


def squares(residual):
    return lax.psum(jnp.sum(residual * residual, axis=0), ("gx", "gy", "nd"))


def shards(right_side, node_diag, local_coup, block_cols, border_coup, border_send, border_rows):
    operands = (node_diag, local_coup, block_cols, border_coup, border_send, border_rows)
    solution_field = jnp.zeros_like(right_side)
    residual = right_side
    direction = right_side
    norm_now = squares(residual)
    for step in range(ITERS):
        image = apply_prec(direction, *operands)
        curve = lax.psum(jnp.sum(direction * image, axis=0), ("gx", "gy", "nd"))
        alpha = norm_now / curve
        solution_field = solution_field + alpha * direction
        if step + 1 < ITERS:
            residual = residual - alpha * image
            norm_next = squares(residual)
            direction = residual + norm_next / norm_now * direction
            norm_now = norm_next
    return solution_field


def solution(mesh):
    in_specs = (
        P(("var", "gx", "gy", "nd"), None),
        P(("var", "gx", "gy", "nd")),
        P(("var", "gx", "gy", "nd"), None, None, None),
        P(("gx", "gy", "nd"), None),
        P(("var", "gx", "gy", "nd"), None, None, None),
        P(("gx", "gy", "nd"), None),
        P(("gx", "gy", "nd"), None),
    )
    out_specs = P(("var", "gx", "gy", "nd"), None)
    return jax.shard_map(shards, mesh=mesh, in_specs=in_specs, out_specs=out_specs, check_vma=False)
```

profile of v0, /device:TPU:0, one launch (start us, length us, event | category | flops | bytes accessed | tf_op | source)
XLA Modules:
  0.0 218.6 jit_solution(11470286495793710172)
XLA Ops:
  7.7 2.6 %fusion.95 = f32[2,7,128,256]{3,2,1,0:T(8,128)S(1)} fusion(f32[2,7,128,128]{3,2,1,0:T(8,128)S(1)} %copy-done, f32[2,128,256,1]{2,1,3,0:T(8,128)} %bitcast.156), kind=kOutput, calls=%fused_computation.120 | convolution fusion | flops 704643072 | bytes 3014656 | tf_op jit(solution)/shard_map/bkji,bjc->bkic/dot_general | solution.py:38
  10.4 1.9 fusion
  13.9 2.0 convolution_bitcast_fusion.1
  16.9 4.8 %collective-permute-start.7 = (f32[1,2,128,256]{2,3,1,0:T(8,128)}, f32[1,2,128,256]{2,3,1,0:T(8,128)S(1)}, u32[]{:S(2)}, u32[]{:S(2)}) collective-permute-start(f32[1,2,128,256]{2,3,1,0:T(8,128)} %get-tuple-element.24), channel_id=1, source_target_pairs={{0,2},{1,3},{4,6},{5,7},{8,10},{9,11},{12,14},{13,15},{16,18},{17,... | collective-permute-start | bytes 786440 | tf_op jit(solution)/shard_map/ppermute | solution.py:17
  24.7 2.2 %collective-permute-start.4 = (f32[1,2,128,256]{2,3,1,0:T(8,128)}, f32[1,2,128,256]{2,3,1,0:T(8,128)}, u32[]{:S(2)}, u32[]{:S(2)}) collective-permute-start(f32[1,2,128,256]{2,3,1,0:T(8,128)} %get-tuple-element.23), channel_id=1, source_target_pairs={{4,0},{8,4},{12,8},{0,12},{5,1},{9,5},{13,9},{1,13},{6,2},{10,6},{... | collective-permute-start | bytes 786440 | tf_op jit(solution)/shard_map/ppermute | solution.py:19
  30.2 2.2 all_gather.6
  32.4 1.9 gather_fusion
  35.0 4.6 %collective-permute-start.2 = (f32[1,2,128,256]{3,2,1,0:T(8,128)}, f32[1,2,128,256]{3,2,1,0:T(8,128)S(1)}, u32[]{:S(2)}, u32[]{:S(2)}) collective-permute-start(f32[1,2,128,256]{3,2,1,0:T(8,128)} %get-tuple-element.21), channel_id=1, source_target_pairs={{0,2},{1,3},{4,6},{5,7},{8,10},{9,11},{12,14},{13,15},{16,18},{17,... | collective-permute-start | bytes 786440 | tf_op jit(solution)/shard_map/ppermute | solution.py:17
  40.4 1.8 collective-permute-start.1
  45.8 3.8 %collective-permute-done.1 = f32[1,2,128,256]{3,2,1,0:T(8,128)S(1)} collective-permute-done((f32[1,2,128,256]{3,2,1,0:T(8,128)}, f32[1,2,128,256]{3,2,1,0:T(8,128)S(1)}, u32[]{:S(2)}, u32[]{:S(2)}) %collective-permute-start.1) | collective-permute-done | bytes 262176 | tf_op jit(solution)/shard_map/ppermute | solution.py:19
  49.6 5.0 %collective-permute-done = f32[1,2,128,256]{3,2,1,0:T(8,128)} collective-permute-done((f32[1,2,128,256]{3,2,1,0:T(8,128)}, f32[1,2,128,256]{3,2,1,0:T(8,128)}, u32[]{:S(2)}, u32[]{:S(2)}) %collective-permute-start) | collective-permute-done | bytes 262176 | tf_op jit(solution)/shard_map/ppermute | solution.py:17
  54.6 2.9 %fusion.36 = f32[8,256,128]{2,1,0:T(8,128)S(1)} fusion(f32[2,128,256]{2,1,0:T(8,128)S(1)} %bitcast.170, f32[2,128,256]{2,1,0:T(8,128)S(1)} %bitcast.173, f32[2,128,256]{2,1,0:T(8,128)S(1)} %bitcast.174, f32[2,128,256]{2,1,0:T(8,128)} %bitcast.14, f32[1,8,128,128]{3,2,1,0:T(8,128)S(1)} %copy-done.2), kind=kOutput, calls=%fused_computation.24 | convolution fusion | flops 403439616 | bytes 2621440 | tf_op jit(solution)/shard_map/mij,mjc->mic/dot_general | solution.py:59
  58.9 2.0 fusion.76
  60.9 2.5 %fusion.54 = f32[2,128,256]{2,0,1:T(2,128)} fusion(f32[8,256,128]{1,0,2:T(8,128)} %copy.39, s32[8]{0:T(128)S(1)} %bitcast.185), kind=kOutput, calls=%fused_computation.44 | convolution fusion | flops 6291472 | bytes 1310752 | tf_op jit(solution)/shard_map/nm,mic->nic/dot_general | solution.py:63
  63.4 2.5 %fusion.33 = f32[2,128,256]{2,1,0:T(8,128)S(1)} fusion(f32[2,128,256]{2,1,0:T(8,128)} %reduce-scatter.3.cloned.1.call-done, f32[2,7,128,128]{3,2,1,0:T(8,128)S(1)} %copy-done, f32[2,7,128,256]{3,2,1,0:T(8,128)S(1)} %bitcast.167, pred[2,7]{1,0:T(4,128)(4,1)} %compare_and_fusion.2, f32[2,128,256]{2,0,1:T(2,128)S(1)} %fusion.76, f32[2,128,256]{2,0,1:T(2,128)} %fusion.54, ...), kind=kOutput, calls=%fused_computation.23 | convolution fusion | flops 705429504 | bytes 4064270 | tf_op jit(solution)/shard_map/bkij,bkjc->bic/dot_general | solution.py:36
  66.0 29.5 %all-reduce = (f32[256]{0:T(256)S(1)}, f32[256]{0:T(256)S(1)}) all-reduce(f32[256]{0:T(256)S(1)} %get-tuple-element.8, f32[256]{0:T(256)S(1)} %get-tuple-element.6), channel_id=1, replica_groups=mesh['var'=2,'gx'=4,'gy'=2,'nd'=2] {'gx','gy','nd'}, use_global_device_ids=true, to_apply=%region_1.0 | all-reduce | flops 512 | bytes 4096 | tf_op jit(solution)/shard_map/psum | solution.py:72
  95.6 29.5 %psum.30 = f32[256]{0:T(256)S(1)} all-reduce(f32[256]{0:T(256)S(1)} %multiply_reduce_fusion), channel_id=1, replica_groups=mesh['var'=2,'gx'=4,'gy'=2,'nd'=2] {'gx','gy','nd'}, use_global_device_ids=true, to_apply=%region_6.9 | all-reduce | flops 256 | bytes 2048 | tf_op jit(solution)/shard_map/psum | solution.py:72
  126.8 1.7 gather_fusion.4
  128.5 2.9 %fusion.96 = f32[2,256,7,128]{3,1,2,0:T(8,128)} fusion(f32[2,128,256,1]{2,1,3,0:T(8,128)S(1)} %bitcast.163, f32[2,7,128,128]{3,2,1,0:T(8,128)S(1)} %copy-done), kind=kOutput, calls=%fused_computation.121 | convolution fusion | flops 704643072 | bytes 3014656 | tf_op jit(solution)/shard_map/bkji,bjc->bkic/dot_general | solution.py:38
  131.4 2.3 %copy.30 = f32[14,128,256]{2,0,1:T(8,128)S(1)} copy(f32[14,128,256]{1,2,0:T(8,128)} %bitcast.169) | data formatting | bytes 3670016 | tf_op jit(solution)/shard_map/reshape | solution.py:38
  136.0 2.7 %convolution_bitcast_fusion = f32[8,128,256]{1,2,0:T(8,128)S(1)} fusion(f32[8,128,256]{2,1,0:T(8,128)S(1)} %copy-done.7, f32[1,8,128,128]{3,2,1,0:T(8,128)S(1)} %copy-done.3, pred[8]{0:T(512)(128)(4,1)} %copy-done.24), kind=kOutput, calls=%fused_computation.12 | convolution fusion | flops 402915328 | bytes 2621448 | tf_op jit(solution)/shard_map/mji,mjc->mic/dot_general | solution.py:51
  141.5 3.8 %collective-permute-start.12 = (f32[1,2,128,256]{2,3,1,0:T(8,128)S(1)}, f32[1,2,128,256]{2,3,1,0:T(8,128)}, u32[]{:S(2)}, u32[]{:S(2)}) collective-permute-start(f32[1,2,128,256]{2,3,1,0:T(8,128)S(1)} %get-tuple-element.15), channel_id=1, source_target_pairs={{4,0},{8,4},{12,8},{0,12},{5,1},{9,5},{13,9},{1,13},{6,2},{10,6},{... | collective-permute-start | bytes 786440 | tf_op jit(solution)/shard_map/ppermute | solution.py:19
  147.8 4.6 %collective-permute-start.10 = (f32[1,2,128,256]{3,2,1,0:T(8,128)}, f32[1,2,128,256]{3,2,1,0:T(8,128)S(1)}, u32[]{:S(2)}, u32[]{:S(2)}) collective-permute-start(f32[1,2,128,256]{3,2,1,0:T(8,128)} %get-tuple-element.13), channel_id=1, source_target_pairs={{0,2},{1,3},{4,6},{5,7},{8,10},{9,11},{12,14},{13,15},{16,18},{17,... | collective-permute-start | bytes 786440 | tf_op jit(solution)/shard_map/ppermute | solution.py:17
  153.2 2.0 collective-permute-start.8
  155.2 2.4 %all_gather.7 = f32[4,128,256]{2,1,0:T(8,128)S(1)} all-gather(f32[2,128,256]{2,1,0:T(8,128)S(1)} %bitcast.164), channel_id=1, replica_groups=mesh['var'=2,'gx'=4,'gy'=2,'nd'=2] {'nd'}, dimensions={0}, use_global_device_ids=true | all-gather | bytes 786432 | tf_op jit(solution)/shard_map/all_gather | solution.py:33
  157.6 1.9 gather_fusion.3
  162.2 6.2 %collective-permute-done.8 = f32[1,2,128,256]{3,2,1,0:T(8,128)} collective-permute-done((f32[1,2,128,256]{3,2,1,0:T(8,128)}, f32[1,2,128,256]{3,2,1,0:T(8,128)}, u32[]{:S(2)}, u32[]{:S(2)}) %collective-permute-start.8) | collective-permute-done | bytes 262176 | tf_op jit(solution)/shard_map/ppermute | solution.py:17
  168.4 3.0 %fusion.44 = f32[8,256,128]{2,1,0:T(8,128)S(1)} fusion(f32[2,128,256]{2,1,0:T(8,128)S(1)} %bitcast.171, f32[2,128,256]{2,1,0:T(8,128)S(1)} %bitcast.172, f32[2,128,256]{2,1,0:T(8,128)} %bitcast.45, f32[2,128,256]{2,1,0:T(8,128)} %bitcast.43, f32[1,8,128,128]{3,2,1,0:T(8,128)S(1)} %copy-done.3), kind=kOutput, calls=%fused_computation.33 | convolution fusion | flops 403439616 | bytes 2621440 | tf_op jit(solution)/shard_map/mij,mjc->mic/dot_general | solution.py:59
  172.8 2.0 fusion.74
  174.7 2.5 %fusion.52 = f32[2,128,256]{2,0,1:T(2,128)} fusion(f32[8,256,128]{1,0,2:T(8,128)} %copy.43, s32[8]{0:T(128)} %bitcast.184), kind=kOutput, calls=%fused_computation.42 | convolution fusion | flops 6291472 | bytes 1310752 | tf_op jit(solution)/shard_map/nm,mic->nic/dot_general | solution.py:63
  177.3 2.6 %fusion.21 = f32[2,128,256]{2,1,0:T(8,128)S(1)} fusion(f32[2,128,256]{2,1,0:T(8,128)} %reduce-scatter.5.cloned.1.call-done, f32[2,7,128,128]{3,2,1,0:T(8,128)S(1)} %copy-done, f32[2,7,128,256]{3,2,1,0:T(8,128)S(1)} %bitcast.168, pred[2,7]{1,0:T(4,128)(4,1)} %compare_and_fusion.2, f32[2,128,256]{2,0,1:T(2,128)S(1)} %fusion.74, f32[2,128,256]{2,0,1:T(2,128)} %fusion.52, ...), kind=kOutput, calls=%fused_computation.19 | convolution fusion | flops 705429504 | bytes 4064270 | tf_op jit(solution)/shard_map/bkij,bkjc->bic/dot_general | solution.py:36
  179.9 31.1 %psum.31 = f32[256]{0:T(256)S(1)} all-reduce(f32[256]{0:T(256)S(1)} %fusion.70), channel_id=1, replica_groups=mesh['var'=2,'gx'=4,'gy'=2,'nd'=2] {'gx','gy','nd'}, use_global_device_ids=true, to_apply=%region_9.12 | all-reduce | flops 256 | bytes 2048 | tf_op jit(solution)/shard_map/psum | solution.py:83
  (119 shorter events, 31.4 us)
Async XLA Ops:
  6.5 56.9 %reduce-scatter.3.cloned.1.call-start = ((), (), s32[]{:S(2)}) async-start(), calls=%async_computation.2 | async-start | bytes 786432 | tf_op jit(solution)/shard_map/reduce_scatter | solution.py:46
  7.4 2.9 %copy-start.22 = (s32[14]{0:T(128)}, s32[14]{0:T(128)S(1)}, u32[]{:S(2)}) copy-start(s32[14]{0:T(128)S(1)} %eq.22) | copy-start | bytes 172
  10.3 2.9 %copy-start.18 = (s32[1,8]{1,0:T(1,128)S(1)}, s32[1,8]{1,0:T(1,128)}, u32[]{:S(2)}) copy-start(s32[1,8]{1,0:T(1,128)} %param.17) | copy-start | bytes 100
  10.3 2.9 %copy-start.1 = (f32[256,256]{1,0:T(8,128)S(1)}, f32[256,256]{1,0:T(8,128)}, u32[]{:S(2)}) copy-start(f32[256,256]{1,0:T(8,128)} %param.11) | copy-start | bytes 786436
  13.1 164.1 %reduce-scatter.5.cloned.1.call-start = ((), (), s32[]{:S(2)}) async-start(), calls=%async_computation.3 | async-start | bytes 786432 | tf_op jit(solution)/shard_map/reduce_scatter | solution.py:46
  13.9 13.1 %copy-start.16 = (s32[1,8]{1,0:T(1,128)S(1)}, s32[1,8]{1,0:T(1,128)}, u32[]{:S(2)}) copy-start(s32[1,8]{1,0:T(1,128)} %param.16) | copy-start | bytes 100
  16.9 17.4 %collective-permute-start.7 = (f32[1,2,128,256]{2,3,1,0:T(8,128)}, f32[1,2,128,256]{2,3,1,0:T(8,128)S(1)}, u32[]{:S(2)}, u32[]{:S(2)}) collective-permute-start(f32[1,2,128,256]{2,3,1,0:T(8,128)} %get-tuple-element.24), channel_id=1, source_target_pairs={{0,2},{1,3},{4,6},{5,7},{8,10},{9,11},{12,14},{13,15},{16,18},{17,... | collective-permute-start | bytes 786440 | tf_op jit(solution)/shard_map/ppermute | solution.py:17
  21.8 17.9 %collective-permute-start.6 = (f32[1,2,128,256]{2,3,1,0:T(8,128)}, f32[1,2,128,256]{2,3,1,0:T(8,128)S(1)}, u32[]{:S(2)}, u32[]{:S(2)}) collective-permute-start(f32[1,2,128,256]{2,3,1,0:T(8,128)} %get-tuple-element.25), channel_id=1, source_target_pairs={{2,0},{3,1},{6,4},{7,5},{10,8},{11,9},{14,12},{15,13},{18,16},{19,... | collective-permute-start | bytes 786440 | tf_op jit(solution)/shard_map/ppermute | solution.py:19
  23.1 19.1 %collective-permute-start.5 = (f32[1,2,128,256]{2,3,1,0:T(8,128)}, f32[1,2,128,256]{2,3,1,0:T(8,128)}, u32[]{:S(2)}, u32[]{:S(2)}) collective-permute-start(f32[1,2,128,256]{2,3,1,0:T(8,128)} %get-tuple-element.26), channel_id=1, source_target_pairs={{0,4},{4,8},{8,12},{12,0},{1,5},{5,9},{9,13},{13,1},{2,6},{6,10},{... | collective-permute-start | bytes 786440 | tf_op jit(solution)/shard_map/ppermute | solution.py:17
  24.7 18.2 %collective-permute-start.4 = (f32[1,2,128,256]{2,3,1,0:T(8,128)}, f32[1,2,128,256]{2,3,1,0:T(8,128)}, u32[]{:S(2)}, u32[]{:S(2)}) collective-permute-start(f32[1,2,128,256]{2,3,1,0:T(8,128)} %get-tuple-element.23), channel_id=1, source_target_pairs={{4,0},{8,4},{12,8},{0,12},{5,1},{9,5},{13,9},{1,13},{6,2},{10,6},{... | collective-permute-start | bytes 786440 | tf_op jit(solution)/shard_map/ppermute | solution.py:19
  28.8 16.8 %collective-permute-start.3 = (f32[1,2,128,256]{3,2,1,0:T(8,128)}, f32[1,2,128,256]{3,2,1,0:T(8,128)S(1)}, u32[]{:S(2)}, u32[]{:S(2)}) collective-permute-start(f32[1,2,128,256]{3,2,1,0:T(8,128)} %get-tuple-element.20), channel_id=1, source_target_pairs={{2,0},{3,1},{6,4},{7,5},{10,8},{11,9},{14,12},{15,13},{18,16},{19,... | collective-permute-start | bytes 786440 | tf_op jit(solution)/shard_map/ppermute | solution.py:19
  32.4 10.0 %copy-start.26 = (s32[2,7]{1,0:T(2,128)S(1)}, s32[2,7]{1,0:T(2,128)}, u32[]{:S(2)}) copy-start(s32[2,7]{1,0:T(2,128)} %param.14) | copy-start | bytes 172
  35.0 10.7 %collective-permute-start.2 = (f32[1,2,128,256]{3,2,1,0:T(8,128)}, f32[1,2,128,256]{3,2,1,0:T(8,128)S(1)}, u32[]{:S(2)}, u32[]{:S(2)}) collective-permute-start(f32[1,2,128,256]{3,2,1,0:T(8,128)} %get-tuple-element.21), channel_id=1, source_target_pairs={{0,2},{1,3},{4,6},{5,7},{8,10},{9,11},{12,14},{13,15},{16,18},{17,... | collective-permute-start | bytes 786440 | tf_op jit(solution)/shard_map/ppermute | solution.py:17
  40.4 9.2 %collective-permute-start.1 = (f32[1,2,128,256]{3,2,1,0:T(8,128)}, f32[1,2,128,256]{3,2,1,0:T(8,128)S(1)}, u32[]{:S(2)}, u32[]{:S(2)}) collective-permute-start(f32[1,2,128,256]{3,2,1,0:T(8,128)} %get-tuple-element.22), channel_id=1, source_target_pairs={{4,0},{8,4},{12,8},{0,12},{5,1},{9,5},{13,9},{1,13},{6,2},{10,6},{... | collective-permute-start | bytes 786440 | tf_op jit(solution)/shard_map/ppermute | solution.py:19
  42.2 12.4 %collective-permute-start = (f32[1,2,128,256]{3,2,1,0:T(8,128)}, f32[1,2,128,256]{3,2,1,0:T(8,128)}, u32[]{:S(2)}, u32[]{:S(2)}) collective-permute-start(f32[1,2,128,256]{3,2,1,0:T(8,128)} %get-tuple-element.19), channel_id=1, source_target_pairs={{0,4},{4,8},{8,12},{12,0},{1,5},{5,9},{9,13},{13,1},{2,6},{6,10},{... | collective-permute-start | bytes 786440 | tf_op jit(solution)/shard_map/ppermute | solution.py:17
  57.5 3.4 %copy-start.19 = (s32[1,8]{1,0:T(1,128)S(1)}, s32[1,8]{1,0:T(1,128)}, u32[]{:S(2)}) copy-start(s32[1,8]{1,0:T(1,128)} %param.17) | copy-start | bytes 100
  58.9 4.5 %copy-start.4 = (f32[14,128,256]{2,1,0:T(8,128)S(1)}, f32[14,128,256]{2,1,0:T(8,128)}, u32[]{:S(2)}) copy-start(f32[14,128,256]{2,1,0:T(8,128)} %gather_fusion) | copy-start | bytes 5505028
  58.9 4.5 %copy-start.14 = (f32[256]{0:T(256)S(1)}, f32[256]{0:T(256)}, u32[]{:S(2)}) copy-start(f32[256]{0:T(256)} %param.12) | copy-start | bytes 3076
  136.0 9.3 %copy-start.6 = (f32[8,128,256]{2,1,0:T(8,128)S(1)}, f32[8,128,256]{2,1,0:T(8,128)}, u32[]{:S(2)}) copy-start(f32[8,128,256]{2,1,0:T(8,128)} %gather_fusion.4) | copy-start | bytes 3145732
  136.0 9.3 %copy-start.21 = (pred[8]{0:T(512)(128)(4,1)S(1)}, pred[8]{0:T(512)(128)(4,1)}, u32[]{:S(2)}) copy-start(pred[8]{0:T(512)(128)(4,1)} %copy-done.20) | copy-start | bytes 28
  138.8 9.0 %collective-permute-start.15 = (f32[1,2,128,256]{2,3,1,0:T(8,128)S(1)}, f32[1,2,128,256]{2,3,1,0:T(8,128)S(1)}, u32[]{:S(2)}, u32[]{:S(2)}) collective-permute-start(f32[1,2,128,256]{2,3,1,0:T(8,128)S(1)} %get-tuple-element.16), channel_id=1, source_target_pairs={{0,2},{1,3},{4,6},{5,7},{8,10},{9,11},{12,14},{13,15},{16,18},{17,... | collective-permute-start | bytes 786440 | tf_op jit(solution)/shard_map/ppermute | solution.py:17
  140.1 12.3 %collective-permute-start.14 = (f32[1,2,128,256]{2,3,1,0:T(8,128)S(1)}, f32[1,2,128,256]{2,3,1,0:T(8,128)S(1)}, u32[]{:S(2)}, u32[]{:S(2)}) collective-permute-start(f32[1,2,128,256]{2,3,1,0:T(8,128)S(1)} %get-tuple-element.17), channel_id=1, source_target_pairs={{2,0},{3,1},{6,4},{7,5},{10,8},{11,9},{14,12},{15,13},{18,16},{19,... | collective-permute-start | bytes 786440 | tf_op jit(solution)/shard_map/ppermute | solution.py:19
  141.4 11.1 %collective-permute-start.13 = (f32[1,2,128,256]{2,3,1,0:T(8,128)S(1)}, f32[1,2,128,256]{2,3,1,0:T(8,128)S(1)}, u32[]{:S(2)}, u32[]{:S(2)}) collective-permute-start(f32[1,2,128,256]{2,3,1,0:T(8,128)S(1)} %get-tuple-element.18), channel_id=1, source_target_pairs={{0,4},{4,8},{8,12},{12,0},{1,5},{5,9},{9,13},{13,1},{2,6},{6,10},{... | collective-permute-start | bytes 786440 | tf_op jit(solution)/shard_map/ppermute | solution.py:17
  141.5 18.0 %collective-permute-start.12 = (f32[1,2,128,256]{2,3,1,0:T(8,128)S(1)}, f32[1,2,128,256]{2,3,1,0:T(8,128)}, u32[]{:S(2)}, u32[]{:S(2)}) collective-permute-start(f32[1,2,128,256]{2,3,1,0:T(8,128)S(1)} %get-tuple-element.15), channel_id=1, source_target_pairs={{4,0},{8,4},{12,8},{0,12},{5,1},{9,5},{13,9},{1,13},{6,2},{10,6},{... | collective-permute-start | bytes 786440 | tf_op jit(solution)/shard_map/ppermute | solution.py:19
  146.5 15.7 %collective-permute-start.11 = (f32[1,2,128,256]{3,2,1,0:T(8,128)}, f32[1,2,128,256]{3,2,1,0:T(8,128)S(1)}, u32[]{:S(2)}, u32[]{:S(2)}) collective-permute-start(f32[1,2,128,256]{3,2,1,0:T(8,128)} %get-tuple-element.12), channel_id=1, source_target_pairs={{2,0},{3,1},{6,4},{7,5},{10,8},{11,9},{14,12},{15,13},{18,16},{19,... | collective-permute-start | bytes 786440 | tf_op jit(solution)/shard_map/ppermute | solution.py:19
  147.8 11.7 %copy-start.10 = (f32[1,2,128,256]{2,3,1,0:T(8,128)}, f32[1,2,128,256]{2,3,1,0:T(8,128)S(1)}, u32[]{:S(2)}) copy-start(f32[1,2,128,256]{2,3,1,0:T(8,128)S(1)} %collective-permute-done.15) | copy-start | bytes 786436
  147.8 14.4 %collective-permute-start.10 = (f32[1,2,128,256]{3,2,1,0:T(8,128)}, f32[1,2,128,256]{3,2,1,0:T(8,128)S(1)}, u32[]{:S(2)}, u32[]{:S(2)}) collective-permute-start(f32[1,2,128,256]{3,2,1,0:T(8,128)} %get-tuple-element.13), channel_id=1, source_target_pairs={{0,2},{1,3},{4,6},{5,7},{8,10},{9,11},{12,14},{13,15},{16,18},{17,... | collective-permute-start | bytes 786440 | tf_op jit(solution)/shard_map/ppermute | solution.py:17
  152.4 9.8 %collective-permute-start.9 = (f32[1,2,128,256]{3,2,1,0:T(8,128)}, f32[1,2,128,256]{3,2,1,0:T(8,128)}, u32[]{:S(2)}, u32[]{:S(2)}) collective-permute-start(f32[1,2,128,256]{3,2,1,0:T(8,128)} %get-tuple-element.14), channel_id=1, source_target_pairs={{4,0},{8,4},{12,8},{0,12},{5,1},{9,5},{13,9},{1,13},{6,2},{10,6},{... | collective-permute-start | bytes 786440 | tf_op jit(solution)/shard_map/ppermute | solution.py:19
  153.2 15.2 %collective-permute-start.8 = (f32[1,2,128,256]{3,2,1,0:T(8,128)}, f32[1,2,128,256]{3,2,1,0:T(8,128)}, u32[]{:S(2)}, u32[]{:S(2)}) collective-permute-start(f32[1,2,128,256]{3,2,1,0:T(8,128)} %get-tuple-element.11), channel_id=1, source_target_pairs={{0,4},{4,8},{8,12},{12,0},{1,5},{5,9},{9,13},{13,1},{2,6},{6,10},{... | collective-permute-start | bytes 786440 | tf_op jit(solution)/shard_map/ppermute | solution.py:17
  168.4 4.4 %copy-start.17 = (s32[1,8]{1,0:T(1,128)S(1)}, s32[1,8]{1,0:T(1,128)}, u32[]{:S(2)}) copy-start(s32[1,8]{1,0:T(1,128)} %param.16) | copy-start | bytes 100
  172.8 4.5 %copy-start.5 = (f32[14,128,256]{2,1,0:T(8,128)S(1)}, f32[14,128,256]{2,1,0:T(8,128)}, u32[]{:S(2)}) copy-start(f32[14,128,256]{2,1,0:T(8,128)} %gather_fusion.3) | copy-start | bytes 5505028
  172.8 4.5 %copy-start.15 = (f32[256]{0:T(256)S(1)}, f32[256]{0:T(256)}, u32[]{:S(2)}) copy-start(f32[256]{0:T(256)} %param.12) | copy-start | bytes 3076
  (13 other events, 17.6 us)
Sparse Core Ops, SparseCore 0:
  13.3 10.6 reduce-scatter.2
  135.5 5.2 reduce-scatter.4
where the time goes:
time: 219 us
  blocking collectives  94.6 us (43%)
  matrix products  32.8 us (15%)
  starting transfers between devices  32.3 us (15%)
  local copies, waits for them, and re-layouts  25.3 us (12%)
  waiting for transfers between devices  15.3 us (7%)
  between operations  13.9 us (6%)
  other arithmetic  4.4 us (2%)
    psum x2, blocking collectives, squares(): return lax.psum(jnp.sum(residual * residual, axis=0), ('gx', 'gy', 'nd'))  59 us
    psum x1, blocking collectives, shards(): curve = lax.psum(jnp.sum(direction * image, axis=0), ('gx', 'gy', 'nd'))  31.1 us
    ppermute x8, starting transfers between devices, with_halo(): lax.ppermute(tail, axis, [(i, (i + 1) % count) for i in range(ends)])  19.2 us
    ppermute x8, starting transfers between devices, with_halo(): lax.ppermute(head, axis, [((i + 1) % count, i) for i in range(ends)])  13.1 us
    ppermute x8, waiting for transfers between devices, with_halo(): lax.ppermute(tail, axis, [(i, (i + 1) % count) for i in range(ends)])  11.4 us
    dot_general x2, matrix products, apply_prec(): contrib = jnp.einsum('mij,mjc->mic', border_coup[0], received, precision=hp)  5.89 us
    dot_general x2, matrix products, apply_prec(): jnp.einsum('bkji,bjc->bkic', local_coup, blocks, precision=hp)  5.47 us
    dot_general x2, matrix products, apply_prec(): jnp.einsum('bkij,bkjc->bic', local_coup, picked, precision=hp)  5.09 us
  transfers between devices with their start and end apart: 18, of which 4 were waited for; matrix products, arithmetic and copies ran while one was open for 17% of the time, Pallas kernels for 0%

commit v1 on v0

v1 whole, which is shorter than its diff:
```python
import functools

import jax
import jax.numpy as jnp
from jax import lax
from jax.experimental import pallas as pl
from jax.experimental.pallas import tpu as pltpu
from jax.sharding import PartitionSpec as P

HP = lax.Precision.HIGHEST
LEFT, RIGHT, DOWN, UP = range(4)
OPPOSITE = (RIGHT, LEFT, UP, DOWN)


def mm(a, b):
    return jnp.dot(a, b, precision=HP, preferred_element_type=jnp.float32)


def kernel(
    sizes,
    rhs, diag, local, cols, border, send, rows,
    out,
    fields, images, local_v, border_v, border_in, pair_out, pair_in, marks, marks_in,
    prec, acc, sums,
    load_sem, f_send, f_recv, m_send, m_recv, k_send, k_recv, p_send, p_recv,
    w_send, w_recv, s_send, s_recv,
):
    nx, ny, nn = sizes
    total = nx * ny * nn
    nb, nnz, bs, _ = local_v.shape
    per = border_v.shape[0] // 4
    size, width = out.shape
    gx, gy, nd = lax.axis_index("gx"), lax.axis_index("gy"), lax.axis_index("nd")
    me = (gx * ny + gy) * nn + nd
    low = gy > 0
    high = gy < ny - 1
    targets = (
        {"gx": lax.rem(gx + nx - 1, nx)},
        {"gx": lax.rem(gx + 1, nx)},
        {"gy": jnp.maximum(gy - 1, 0)},
        {"gy": jnp.minimum(gy + 1, ny - 1)},
    )
    partner = {"nd": 1 - nd}

    def peer(step):
        other = lax.rem(me + step, total)
        return {"gx": other // (ny * nn), "gy": lax.rem(other // nn, ny), "nd": lax.rem(other, nn)}

    def over_peers(body):
        if total <= 16:
            for step in range(1, total):
                body(step)
        else:
            lax.fori_loop(1, total, lambda step, _: (body(step), 0)[1], 0)

    def side(turn, body):
        if turn == DOWN:
            pl.when(low)(body)
        elif turn == UP:
            pl.when(high)(body)
        else:
            body()

    def remote(src, dst, ssem, rsem, where):
        return pltpu.make_async_remote_copy(
            src_ref=src, dst_ref=dst, send_sem=ssem, recv_sem=rsem,
            device_id=where, device_id_type=pl.DeviceIdType.MESH,
        )

    loads = [
        pltpu.make_async_copy(local, local_v, load_sem.at[0]),
        pltpu.make_async_copy(rhs, fields.at[0], load_sem.at[1]),
        pltpu.make_async_copy(border.at[0], border_v, load_sem.at[2]),
    ]
    for load in loads:
        load.start()

    barrier = pltpu.get_barrier_semaphore()
    over_peers(
        lambda step: pl.semaphore_signal(
            barrier, inc=1, device_id=peer(step), device_id_type=pl.DeviceIdType.MESH
        )
    )
    for m in range(4 * per):
        marks[m : m + 1, :] = jnp.full((1, 128), send[0, m], jnp.int32).astype(jnp.float32)
        at = 4 * per + m
        marks[at : at + 1, :] = jnp.full((1, 128), rows[0, m], jnp.int32).astype(jnp.float32)
    pl.semaphore_wait(barrier, total - 1)

    def mark_copy(turn):
        opp = OPPOSITE[turn]
        return remote(marks, marks_in.at[opp], k_send.at[turn], k_recv.at[opp], targets[turn])

    def border_copy(turn):
        opp = OPPOSITE[turn]
        return remote(
            border.at[0, pl.ds(turn * per, per)], border_in.at[opp],
            m_send.at[turn], m_recv.at[opp], targets[turn],
        )

    def field_copy(turn):
        opp = OPPOSITE[turn]
        return remote(rhs, fields.at[2 + opp], f_send.at[turn], f_recv.at[opp], targets[turn])

    for make in (mark_copy, border_copy, field_copy):
        for turn in range(4):
            side(turn, lambda: make(turn).start())
    field_pair = remote(rhs, fields.at[1], f_send.at[4], f_recv.at[4], partner)
    field_pair.start()

    loads[0].wait()
    for i in range(nb):
        for j in range(nb):
            own = jnp.zeros((bs, bs), jnp.float32)
            far = jnp.zeros((bs, bs), jnp.float32)
            for k in range(nnz):
                block = local_v[i, k]
                col = cols[i, k]
                own = own + jnp.where(col == nd * nb + j, 1.0, 0.0) * block
                far = far + jnp.where(col == (1 - nd) * nb + j, 1.0, 0.0) * block
            prec[0, i * bs : (i + 1) * bs, j * bs : (j + 1) * bs] = own
            pair_out[i * bs : (i + 1) * bs, j * bs : (j + 1) * bs] = far
    pair = remote(pair_out, pair_in, p_send, p_recv, partner)
    pair.start()
    prec[0] = prec[0] + prec[0].T

    eye = lax.broadcasted_iota(jnp.int32, (size, size), 0) == lax.broadcasted_iota(
        jnp.int32, (size, size), 1
    )
    column = jnp.sum(
        jnp.where(eye, jnp.broadcast_to(diag[...], (size, size)), 0.0), axis=1, keepdims=True
    )

    loads[1].wait()
    acc[...] = column * fields[0] + mm(prec[0], fields[0])
    pair.wait()
    prec[1] = pair_out[...] + pair_in[...].T
    field_pair.wait()
    acc[...] += mm(prec[1], fields[1])

    loads[2].wait()

    def couple(turn):
        opp = OPPOSITE[turn]
        mark_copy(turn).wait_send()
        border_copy(turn).wait_send()
        remote(marks, marks_in.at[turn], k_send.at[turn], k_recv.at[turn], targets[turn]).wait_recv()
        remote(
            border.at[0, pl.ds(turn * per, per)], border_in.at[turn],
            m_send.at[turn], m_recv.at[turn], targets[turn],
        ).wait_recv()
        back = [border_in[turn, s].T for s in range(per)]
        for i in range(nb):
            for j in range(nb):
                block = jnp.zeros((bs, bs), jnp.float32)
                for s in range(per):
                    m, n = turn * per + s, opp * per + s
                    to = jnp.where(rows[0, m] == i, 1.0, 0.0)
                    took = jnp.where(marks_in[turn, m : m + 1, :] == float(j), 1.0, 0.0)
                    block = block + (to * took) * border_v[m]
                    to = jnp.where(send[0, n] == i, 1.0, 0.0)
                    at = 4 * per + n
                    took = jnp.where(marks_in[turn, at : at + 1, :] == float(j), 1.0, 0.0)
                    block = block + (to * took) * back[s]
                prec[2 + turn, i * bs : (i + 1) * bs, j * bs : (j + 1) * bs] = block

    def join(turn):
        field_copy(turn).wait_send()
        remote(
            rhs, fields.at[2 + turn], f_send.at[turn], f_recv.at[turn], targets[turn]
        ).wait_recv()
        acc[...] += mm(prec[2 + turn], fields[2 + turn])

    for turn in (DOWN, UP, LEFT, RIGHT):
        side(turn, lambda: couple(turn))
    for turn in (DOWN, UP, LEFT, RIGHT):
        side(turn, lambda: join(turn))

    images[0] = acc[...]

    def image_copy(turn, slot):
        where = partner if turn is None else targets[turn]
        return remote(images.at[0], images.at[slot], w_send.at[slot - 1], w_recv.at[slot - 1], where)

    image_copy(RIGHT, 2).start()
    side(UP, lambda: image_copy(UP, 3).start())
    image_copy(None, 1).start()

    def share(phase, first, second):
        sums[phase, me, 0:1, :] = first
        sums[phase, me, 1:2, :] = second
        over_peers(
            lambda step: remote(
                sums.at[phase, me], sums.at[phase, me], s_send.at[phase], s_recv.at[phase],
                peer(step),
            ).start()
        )

    def collect(phase):
        every = sums.at[phase, pl.ds(0, total - 1)]
        done = remote(every, every, s_send.at[phase], s_recv.at[phase], partner)
        done.wait_send()
        done.wait_recv()
        both = jnp.sum(sums[phase], axis=0)
        return both[0:1, :], both[1:2, :]

    def column_sum(a):
        return jnp.sum(a, axis=0, keepdims=True)

    share(0, column_sum(fields[0] * fields[0]), column_sum(fields[0] * images[0]))
    norm, curve = collect(0)
    alpha = norm / curve

    acc[...] = fields[0] - alpha * images[0]
    image_copy(None, 1).wait()
    far = fields[1] - alpha * images[1]
    images[1] = column * acc[...] + mm(prec[0], acc[...]) + mm(prec[1], far)

    def add_below():
        image_copy(UP, 3).wait_recv()
        images[1] += 2.0 * mm(prec[2 + DOWN], fields[2 + DOWN] - alpha * images[3])

    side(DOWN, add_below)
    side(UP, lambda: image_copy(UP, 3).wait_send())
    image_copy(RIGHT, 2).wait()
    images[1] += 2.0 * mm(prec[2 + LEFT], fields[2 + LEFT] - alpha * images[2])
    share(1, column_sum(acc[...] * acc[...]), column_sum(acc[...] * images[1]))
    norm_next, quad = collect(1)
    ratio = norm_next / norm
    alpha_next = norm_next / (quad - ratio * norm_next / alpha)
    out[...] = alpha * fields[0] + alpha_next * (acc[...] + ratio * fields[0])


def shards(sizes, right_side, node_diag, local_coup, block_cols, border_coup, border_send, border_rows):
    size, width = right_side.shape
    nb, nnz, bs, _ = local_coup.shape
    slots = border_coup.shape[1]
    per = slots // 4
    total = sizes[0] * sizes[1] * sizes[2]
    vmem = pl.BlockSpec(memory_space=pltpu.VMEM)
    smem = pl.BlockSpec(memory_space=pltpu.SMEM)
    anywhere = pl.BlockSpec(memory_space=pl.ANY)
    f32 = jnp.float32
    dma = pltpu.SemaphoreType.DMA
    return pl.pallas_call(
        functools.partial(kernel, sizes),
        out_shape=jax.ShapeDtypeStruct((size, width), f32),
        in_specs=[anywhere, vmem, anywhere, smem, anywhere, smem, smem],
        out_specs=vmem,
        scratch_shapes=[
            pltpu.VMEM((6, size, width), f32),
            pltpu.VMEM((4, size, width), f32),
            pltpu.VMEM((nb, nnz, bs, bs), f32),
            pltpu.VMEM((slots, bs, bs), f32),
            pltpu.VMEM((4, per, bs, bs), f32),
            pltpu.VMEM((size, size), f32),
            pltpu.VMEM((size, size), f32),
            pltpu.VMEM((2 * slots, 128), f32),
            pltpu.VMEM((4, 2 * slots, 128), f32),
            pltpu.VMEM((6, size, size), f32),
            pltpu.VMEM((size, width), f32),
            pltpu.VMEM((2, total, 2, width), f32),
            dma((3,)), dma((5,)), dma((5,)), dma((4,)), dma((4,)), dma((4,)), dma((4,)),
            dma, dma, dma((3,)), dma((3,)), dma((2,)), dma((2,)),
        ],
        compiler_params=pltpu.CompilerParams(
            collective_id=0, has_side_effects=True, vmem_limit_bytes=40 * 1024 * 1024
        ),
    )(
        right_side, node_diag.reshape(1, size), local_coup, block_cols, border_coup,
        border_send, border_rows,
    )


def solution(mesh):
    in_specs = (
        P(("var", "gx", "gy", "nd"), None),
        P(("var", "gx", "gy", "nd")),
        P(("var", "gx", "gy", "nd"), None, None, None),
        P(("gx", "gy", "nd"), None),
        P(("var", "gx", "gy", "nd"), None, None, None),
        P(("gx", "gy", "nd"), None),
        P(("gx", "gy", "nd"), None),
    )
    out_specs = P(("var", "gx", "gy", "nd"), None)
    sizes = tuple(mesh.shape[axis] for axis in ("gx", "gy", "nd"))
    return jax.shard_map(
        functools.partial(shards, sizes), mesh=mesh, in_specs=in_specs, out_specs=out_specs,
        check_vma=False,
    )
```

time: 219 us -> 48.3 us (0.22)
  blocking collectives: 94.6 us -> 0 us
  Pallas kernels: 0 us -> 42.1 us
  matrix products: 32.8 us -> 0 us
  starting transfers between devices: 32.3 us -> 0 us
  local copies, waits for them, and re-layouts: 25.3 us -> 5.9 us
  waiting for transfers between devices: 15.3 us -> 0 us
  between operations: 13.9 us -> 0.02 us
  other arithmetic: 4.4 us -> 0 us
    psum x3 -> x0, blocking collectives: 90.1 us -> none  [the longest x2 59 us: squares(): return lax.psum(jnp.sum(residual * residual, axis=0), ('gx', 'gy', 'nd'))]
    pallas_call x0 -> x1, Pallas kernels: none -> 42.1 us  [shards(): pl.pallas_call(functools.partial(kernel, sizes), out_shape=jax.ShapeDtype...]
    dot_general x14 -> x0, matrix products: 32.8 us -> none  [the longest x2 5.89 us: apply_prec(): contrib = jnp.einsum('mij,mjc->mic', border_coup[0], received, precision=hp)]
    ppermute x16 -> x0, starting transfers between devices: 32.3 us -> none  [the longest x8 19.2 us: with_halo(): lax.ppermute(tail, axis, [(i, (i + 1) % count) for i in range(ends)])]
    ppermute x16 -> x0, waiting for transfers between devices: 15.2 us -> none  [the longest x8 11.4 us: with_halo(): lax.ppermute(tail, axis, [(i, (i + 1) % count) for i in range(ends)])]
    gather x6 -> x0, local copies, waits for them, and re-layouts: 8.39 us -> none  [the longest x2 3.84 us: apply_prec(): picked = jnp.take(patch, block_cols, axis=0)]
    dot_general x4 -> x0, local copies, waits for them, and re-layouts: 4.6 us -> none  [the longest x2 2.81 us: apply_prec(): contrib = jnp.einsum('mij,mjc->mic', border_coup[0], received, precision=hp)]
    all_gather x2 -> x0, blocking collectives: 4.56 us -> none  [apply_prec(): patch = lax.all_gather(blocks, 'nd', axis=0, tiled=True)]
  transfers between devices with their start and end apart: 18 -> 0, of which waited for: 4 -> 0; matrix products, arithmetic and copies ran while one was open for 17% -> 0% of each run, Pallas kernels for 0% -> 0%
where the time goes in v1:
time: 48.3 us; the launch traced here: 48 us
  Pallas kernels  42.1 us (87%)
  local copies, waits for them, and re-layouts  5.9 us (12%)
    pallas_call x1, Pallas kernels, shards(): pl.pallas_call(functools.partial(kernel, sizes), out_shape=jax.ShapeDtype...  42.1 us
    unnamed x15, local copies, waits for them, and re-layouts  5.9 us

profile of v1, /device:TPU:0, one launch (start us, length us, event | category | flops | bytes accessed | tf_op | source)
XLA Modules:
  0.0 48.0 jit_solution(2367503293114700940)
XLA Ops:
  0.0 0.0 copy-start.5
  0.0 0.0 copy-start.3
  0.0 0.7 %copy-done.5 = s32[1,8]{1,0:T(1,128)S(1)} copy-done((s32[1,8]{1,0:T(1,128)S(1)}, s32[1,8]{1,0:T(1,128)}, u32[]{:S(2)}) %copy-start.5) | copy-done | bytes 56
  0.7 0.0 copy-done.3
  0.7 0.0 copy-start
  0.7 1.2 %copy-done = f32[2,7,128,128]{3,2,1,0:T(8,128)S(1)} copy-done((f32[2,7,128,128]{3,2,1,0:T(8,128)S(1)}, f32[2,7,128,128]{3,2,1,0:T(8,128)}, u32[]{:S(2)}) %copy-start) | copy-done | bytes 917528
  1.9 0.0 copy-start.1
  1.9 1.0 %copy-done.1 = f32[1,8,128,128]{3,2,1,0:T(8,128)S(1)} copy-done((f32[1,8,128,128]{3,2,1,0:T(8,128)S(1)}, f32[1,8,128,128]{3,2,1,0:T(8,128)}, u32[]{:S(2)}) %copy-start.1) | copy-done | bytes 524312
  2.9 0.0 copy-start.2
  2.9 0.9 %copy-done.2 = f32[256,256]{1,0:T(8,128)S(1)} copy-done((f32[256,256]{1,0:T(8,128)S(1)}, f32[256,256]{1,0:T(8,128)}, u32[]{:S(2)}) %copy-start.2) | copy-done | bytes 262168
  3.9 0.0 copy-start.4
  3.9 0.7 %copy-done.4 = s32[2,7]{1,0:T(2,128)S(1)} copy-done((s32[2,7]{1,0:T(2,128)S(1)}, s32[2,7]{1,0:T(2,128)}, u32[]{:S(2)}) %copy-start.4) | copy-done | bytes 80
  4.5 0.0 copy-start.6
  4.5 0.7 %copy-done.6 = s32[1,8]{1,0:T(1,128)S(1)} copy-done((s32[1,8]{1,0:T(1,128)S(1)}, s32[1,8]{1,0:T(1,128)}, u32[]{:S(2)}) %copy-start.6) | copy-done | bytes 56
  5.2 42.1 %shard_map.73 = f32[256,256]{1,0:T(8,128)S(1)} custom-call(f32[256,256]{1,0:T(8,128)S(1)} %copy-done.2, f32[1,256]{1,0:T(1,128)S(1)} %bitcast.1, f32[2,7,128,128]{3,2,1,0:T(8,128)S(1)} %copy-done, s32[2,7]{1,0:T(2,128)S(1)} %copy-done.4, f32[1,8,128,128]{3,2,1,0:T(8,128)S(1)} %copy-done.1, s32[1,8]{1,0:T(1,128)S(1)} %copy-done.5, s32[1,8]{1,0:T(1,128)S(1)} %copy-done.6), custom_call_target="tpu_custom_call" | custom-call | tf_op jit(solution)/shard_map/pallas_call | solution.py:245
  47.3 0.7 %copy.9 = f32[256,256]{1,0:T(8,128)} copy(f32[256,256]{1,0:T(8,128)S(1)} %shard_map.73) | data formatting | bytes 524288
Async XLA Ops:
  0.0 0.7 %copy-start.5 = (s32[1,8]{1,0:T(1,128)S(1)}, s32[1,8]{1,0:T(1,128)}, u32[]{:S(2)}) copy-start(s32[1,8]{1,0:T(1,128)} %send.1) | copy-start | bytes 100
  0.0 0.7 %copy-start.3 = (f32[256]{0:T(256)S(1)}, f32[256]{0:T(256)}, u32[]{:S(2)}) copy-start(f32[256]{0:T(256)} %param.8) | copy-start | bytes 3076
  0.7 1.2 %copy-start = (f32[2,7,128,128]{3,2,1,0:T(8,128)S(1)}, f32[2,7,128,128]{3,2,1,0:T(8,128)}, u32[]{:S(2)}) copy-start(f32[2,7,128,128]{3,2,1,0:T(8,128)} %local.1) | copy-start | bytes 2752516
  1.9 1.0 %copy-start.1 = (f32[1,8,128,128]{3,2,1,0:T(8,128)S(1)}, f32[1,8,128,128]{3,2,1,0:T(8,128)}, u32[]{:S(2)}) copy-start(f32[1,8,128,128]{3,2,1,0:T(8,128)} %border.1) | copy-start | bytes 1572868
  2.9 0.9 %copy-start.2 = (f32[256,256]{1,0:T(8,128)S(1)}, f32[256,256]{1,0:T(8,128)}, u32[]{:S(2)}) copy-start(f32[256,256]{1,0:T(8,128)} %rhs.1) | copy-start | bytes 786436
  3.9 0.7 %copy-start.4 = (s32[2,7]{1,0:T(2,128)S(1)}, s32[2,7]{1,0:T(2,128)}, u32[]{:S(2)}) copy-start(s32[2,7]{1,0:T(2,128)} %cols.1) | copy-start | bytes 172
  4.5 0.7 %copy-start.6 = (s32[1,8]{1,0:T(1,128)S(1)}, s32[1,8]{1,0:T(1,128)}, u32[]{:S(2)}) copy-start(s32[1,8]{1,0:T(1,128)} %rows.1) | copy-start | bytes 100

commit v2 on v1

v2 whole, which is shorter than its diff:
```python
import functools

import jax
import jax.numpy as jnp
from jax import lax
from jax.experimental import pallas as pl
from jax.experimental.pallas import tpu as pltpu
from jax.sharding import PartitionSpec as P

HP = lax.Precision.HIGHEST
LEFT, RIGHT, DOWN, UP = range(4)
CHUNK = 128


def mm(a, b):
    return jnp.dot(a, b, precision=HP, preferred_element_type=jnp.float32)


def column_sum(a):
    return jnp.sum(a, axis=0, keepdims=True)


def kernel(
    sizes,
    rhs, diag_hbm, local, cols_hbm, border, send_hbm, rows_hbm,
    out,
    fields, images, prods_out, prods_in, local_v, border_v, border_in, pair_out, pair_in,
    marks, marks_in, prec, work, sums, diag, cols, send, rows,
    load_sem, f_send, f_recv, m_send, m_recv, k_send, k_recv, p_send, p_recv,
    b_send, b_recv, w_send, w_recv, s_send, s_recv,
):
    nx, ny, nn = sizes
    total = nx * ny * nn
    nb, nnz, bs, _ = local_v.shape
    per = border_v.shape[0] // 4
    size, width = out.shape
    chunks = width // CHUNK
    gx, gy, nd = lax.axis_index("gx"), lax.axis_index("gy"), lax.axis_index("nd")
    me = (gx * ny + gy) * nn + nd
    low = gy > 0
    high = gy < ny - 1
    left = {"gx": lax.rem(gx + nx - 1, nx)}
    right = {"gx": lax.rem(gx + 1, nx)}
    below = {"gy": jnp.maximum(gy - 1, 0)}
    above = {"gy": jnp.minimum(gy + 1, ny - 1)}
    partner = {"nd": 1 - nd}
    forward = (right, above)
    backward = (left, below)
    has_next = (None, high)
    has_last = (None, low)
    came = (LEFT, DOWN)
    goes = (RIGHT, UP)

    def given(condition, body):
        if condition is None:
            body()
        else:
            pl.when(condition)(body)

    def part(c):
        return pl.ds(c * CHUNK, CHUNK)

    def span(c):
        return slice(c * CHUNK, (c + 1) * CHUNK)

    def peer(step):
        other = lax.rem(me + step, total)
        return {"gx": other // (ny * nn), "gy": lax.rem(other // nn, ny), "nd": lax.rem(other, nn)}

    def over_peers(body):
        if total <= 16:
            for step in range(1, total):
                body(step)
        else:
            lax.fori_loop(1, total, lambda step, _: (body(step), 0)[1], 0)

    def remote(src, dst, ssem, rsem, where):
        return pltpu.make_async_remote_copy(
            src_ref=src, dst_ref=dst, send_sem=ssem, recv_sem=rsem,
            device_id=where, device_id_type=pl.DeviceIdType.MESH,
        )

    pairs = (
        (send_hbm, send), (rows_hbm, rows), (cols_hbm, cols), (local, local_v),
        (border.at[0], border_v), (rhs, fields.at[0]), (diag_hbm, diag),
    )
    loads = [pltpu.make_async_copy(src, dst, load_sem.at[i]) for i, (src, dst) in enumerate(pairs)]
    for load in loads:
        load.start()

    barrier = pltpu.get_barrier_semaphore()
    over_peers(
        lambda step: pl.semaphore_signal(
            barrier, inc=1, device_id=peer(step), device_id_type=pl.DeviceIdType.MESH
        )
    )
    loads[0].wait()
    loads[1].wait()
    for m in range(4 * per):
        marks[m : m + 1, :] = jnp.full((1, 128), send[0, m], jnp.int32).astype(jnp.float32)
        at = 4 * per + m
        marks[at : at + 1, :] = jnp.full((1, 128), rows[0, m], jnp.int32).astype(jnp.float32)
    pl.semaphore_wait(barrier, total - 1)

    mark_copy = [
        remote(marks, marks_in.at[a], k_send.at[a], k_recv.at[a], forward[a]) for a in range(2)
    ]
    border_copy = [
        remote(
            border.at[0, pl.ds(goes[a] * per, per)], border_in.at[a],
            m_send.at[a], m_recv.at[a], forward[a],
        )
        for a in range(2)
    ]
    field_copy = [
        [
            remote(
                rhs.at[:, part(c)], fields.at[2 + a, :, part(c)],
                f_send.at[a, c], f_recv.at[a, c], forward[a],
            )
            for c in range(chunks)
        ]
        for a in range(2)
    ]
    back_copy = [
        [
            remote(
                prods_out.at[a, :, part(c)], prods_in.at[a, :, part(c)],
                b_send.at[a, c], b_recv.at[a, c], backward[a],
            )
            for c in range(chunks)
        ]
        for a in range(2)
    ]
    image_copy = [
        [
            remote(
                images.at[0, :, part(c)], images.at[slot, :, part(c)],
                w_send.at[i, c], w_recv.at[i, c], where,
            )
            for c in range(chunks)
        ]
        for i, (slot, where) in enumerate(((2, right), (3, above), (1, partner)))
    ]
    field_pair = remote(rhs, fields.at[1], f_send.at[2, 0], f_recv.at[2, 0], partner)
    pair = remote(pair_out, pair_in, p_send, p_recv, partner)

    for a in range(2):
        given(has_next[a], lambda: mark_copy[a].start())
    for a in range(2):
        given(has_next[a], lambda: border_copy[a].start())
    for c in range(chunks):
        for a in range(2):
            given(has_next[a], lambda: field_copy[a][c].start())
    field_pair.start()

    loads[2].wait()
    loads[3].wait()
    for i in range(nb):
        for j in range(nb):
            own = jnp.zeros((bs, bs), jnp.float32)
            far = jnp.zeros((bs, bs), jnp.float32)
            for k in range(nnz):
                block = local_v[i, k]
                col = cols[i, k]
                own = own + jnp.where(col == nd * nb + j, 1.0, 0.0) * block
                far = far + jnp.where(col == (1 - nd) * nb + j, 1.0, 0.0) * block
            prec[0, i * bs : (i + 1) * bs, j * bs : (j + 1) * bs] = own
            pair_out[i * bs : (i + 1) * bs, j * bs : (j + 1) * bs] = far
    pair.start()
    prec[0] = prec[0] + prec[0].T

    loads[4].wait()
    loads[5].wait()

    def couple(a):
        mark_copy[a].wait_recv()
        border_copy[a].wait_recv()
        turn, opp = came[a], goes[a]
        back = [border_in[a, s].T for s in range(per)]
        for i in range(nb):
            for j in range(nb):
                block = jnp.zeros((bs, bs), jnp.float32)
                for s in range(per):
                    m, n = turn * per + s, opp * per + s
                    to = jnp.where(rows[0, m] == i, 1.0, 0.0)
                    took = jnp.where(marks_in[a, m : m + 1, :] == float(j), 1.0, 0.0)
                    block = block + (to * took) * border_v[m]
                    to = jnp.where(send[0, n] == i, 1.0, 0.0)
                    at = 4 * per + n
                    took = jnp.where(marks_in[a, at : at + 1, :] == float(j), 1.0, 0.0)
                    block = block + (to * took) * back[s]
                prec[2 + a, i * bs : (i + 1) * bs, j * bs : (j + 1) * bs] = block
        prec[4 + a] = prec[2 + a].T
        for c in range(chunks):
            prods_out[a, :, span(c)] = mm(prec[4 + a], fields[0, :, span(c)])
            back_copy[a][c].start()

    given(has_last[1], lambda: couple(1))
    given(has_last[0], lambda: couple(0))

    loads[6].wait()
    eye = lax.broadcasted_iota(jnp.int32, (size, size), 0) == lax.broadcasted_iota(
        jnp.int32, (size, size), 1
    )
    column = jnp.sum(
        jnp.where(eye, jnp.broadcast_to(diag[...], (size, size)), 0.0), axis=1, keepdims=True
    )
    work[...] = column * fields[0] + mm(prec[0], fields[0])
    pair.wait()
    prec[1] = pair_out[...] + pair_in[...].T
    field_pair.wait()
    work[...] += mm(prec[1], fields[1])

    for c in range(chunks):

        def from_last(a):
            field_copy[a][c].wait_recv()
            work[:, span(c)] += mm(prec[2 + a], fields[2 + a, :, span(c)])

        def from_next(a):
            back_copy[a][c].wait_recv()
            work[:, span(c)] += prods_in[a, :, span(c)]

        for a in (1, 0):
            given(has_last[a], lambda: from_last(a))
            given(has_next[a], lambda: from_next(a))
        images[0, :, span(c)] = work[:, span(c)]
        image_copy[0][c].start()
        given(high, lambda: image_copy[1][c].start())
        image_copy[2][c].start()

    def share(phase, first, second):
        sums[phase, me, 0:1, :] = first
        sums[phase, me, 1:2, :] = second
        over_peers(
            lambda step: remote(
                sums.at[phase, me], sums.at[phase, me], s_send.at[phase], s_recv.at[phase],
                peer(step),
            ).start()
        )

    def collect(phase):
        every = sums.at[phase, pl.ds(0, total - 1)]
        done = remote(every, every, s_send.at[phase], s_recv.at[phase], partner)
        done.wait_send()
        done.wait_recv()
        both = jnp.sum(sums[phase], axis=0)
        return both[0:1, :], both[1:2, :]

    share(0, column_sum(fields[0] * fields[0]), column_sum(fields[0] * images[0]))
    norm, curve = collect(0)
    alpha = norm / curve

    out[...] = fields[0] - alpha * images[0]
    work[...] = column * out[...] + mm(prec[0], out[...])
    for c in range(chunks):

        def quad_last(a):
            image_copy[a][c].wait_recv()
            behind = fields[2 + a, :, span(c)] - alpha[:, span(c)] * images[2 + a, :, span(c)]
            work[:, span(c)] += 2.0 * mm(prec[2 + a], behind)

        image_copy[2][c].wait_recv()
        across = fields[1, :, span(c)] - alpha[:, span(c)] * images[1, :, span(c)]
        work[:, span(c)] += mm(prec[1], across)
        for a in (1, 0):
            given(has_last[a], lambda: quad_last(a))
    share(1, column_sum(out[...] * out[...]), column_sum(out[...] * work[...]))

    for a in range(2):
        given(has_next[a], lambda: mark_copy[a].wait_send())
        given(has_next[a], lambda: border_copy[a].wait_send())
        for c in range(chunks):
            given(has_next[a], lambda: field_copy[a][c].wait_send())
            given(has_last[a], lambda: back_copy[a][c].wait_send())
            given(has_next[a], lambda: image_copy[a][c].wait_send())
    for c in range(chunks):
        image_copy[2][c].wait_send()

    norm_next, quad = collect(1)
    ratio = norm_next / norm
    alpha_next = norm_next / (quad - ratio * norm_next / alpha)
    out[...] = (alpha + alpha_next * ratio) * fields[0] + alpha_next * out[...]


def shards(sizes, right_side, node_diag, local_coup, block_cols, border_coup, border_send, border_rows):
    size, width = right_side.shape
    nb, nnz, bs, _ = local_coup.shape
    slots = border_coup.shape[1]
    per = slots // 4
    total = sizes[0] * sizes[1] * sizes[2]
    chunks = width // CHUNK
    hbm = pl.BlockSpec(memory_space=pltpu.HBM)
    f32 = jnp.float32
    dma = pltpu.SemaphoreType.DMA
    return pl.pallas_call(
        functools.partial(kernel, sizes),
        out_shape=jax.ShapeDtypeStruct((size, width), f32),
        in_specs=[hbm] * 7,
        out_specs=pl.BlockSpec(memory_space=pltpu.VMEM),
        scratch_shapes=[
            pltpu.VMEM((4, size, width), f32),
            pltpu.VMEM((4, size, width), f32),
            pltpu.VMEM((2, size, width), f32),
            pltpu.VMEM((2, size, width), f32),
            pltpu.VMEM((nb, nnz, bs, bs), f32),
            pltpu.VMEM((slots, bs, bs), f32),
            pltpu.VMEM((2, per, bs, bs), f32),
            pltpu.VMEM((size, size), f32),
            pltpu.VMEM((size, size), f32),
            pltpu.VMEM((2 * slots, 128), f32),
            pltpu.VMEM((2, 2 * slots, 128), f32),
            pltpu.VMEM((6, size, size), f32),
            pltpu.VMEM((size, width), f32),
            pltpu.VMEM((2, total, 2, width), f32),
            pltpu.VMEM((1, size), f32),
            pltpu.SMEM((nb, nnz), jnp.int32),
            pltpu.SMEM((1, slots), jnp.int32),
            pltpu.SMEM((1, slots), jnp.int32),
            dma((7,)), dma((3, chunks)), dma((3, chunks)), dma((2,)), dma((2,)), dma((2,)), dma((2,)),
            dma, dma, dma((2, chunks)), dma((2, chunks)), dma((3, chunks)), dma((3, chunks)),
            dma((2,)), dma((2,)),
        ],
        compiler_params=pltpu.CompilerParams(
            collective_id=0, has_side_effects=True, vmem_limit_bytes=48 * 1024 * 1024
        ),
    )(
        right_side, node_diag.reshape(1, size), local_coup, block_cols, border_coup,
        border_send, border_rows,
    )


def solution(mesh):
    in_specs = (
        P(("var", "gx", "gy", "nd"), None),
        P(("var", "gx", "gy", "nd")),
        P(("var", "gx", "gy", "nd"), None, None, None),
        P(("gx", "gy", "nd"), None),
        P(("var", "gx", "gy", "nd"), None, None, None),
        P(("gx", "gy", "nd"), None),
        P(("gx", "gy", "nd"), None),
    )
    out_specs = P(("var", "gx", "gy", "nd"), None)
    sizes = tuple(mesh.shape[axis] for axis in ("gx", "gy", "nd"))
    return jax.shard_map(
        functools.partial(shards, sizes), mesh=mesh, in_specs=in_specs, out_specs=out_specs,
        check_vma=False,
    )
```

time: 48.3 us -> 44.3 us (0.917)
  Pallas kernels: 42.1 us -> 38.1 us
    pallas_call x1, Pallas kernels: 42.1 us -> 38.1 us  [shards(): pl.pallas_call(functools.partial(kernel, sizes), out_shape=jax.ShapeDtype...]
where the time goes in v2:
time: 44.3 us; the launch traced here: 44 us
  Pallas kernels  38.1 us (86%)
  local copies, waits for them, and re-layouts  5.9 us (13%)
    pallas_call x1, Pallas kernels, shards(): pl.pallas_call(functools.partial(kernel, sizes), out_shape=jax.ShapeDtype...  38.1 us
    unnamed x15, local copies, waits for them, and re-layouts  5.9 us

profile of v2, /device:TPU:0, one launch (start us, length us, event | category | flops | bytes accessed | tf_op | source)
XLA Modules:
  0.0 44.0 jit_solution(15799225060111308307)
XLA Ops:
  0.0 0.0 copy-start.5
  0.0 0.0 copy-start.3
  0.0 0.7 %copy-done.5 = s32[1,8]{1,0:T(1,128)S(1)} copy-done((s32[1,8]{1,0:T(1,128)S(1)}, s32[1,8]{1,0:T(1,128)}, u32[]{:S(2)}) %copy-start.5) | copy-done | bytes 56
  0.7 0.0 copy-done.3
  0.7 0.0 copy-start
  0.7 1.2 %copy-done = f32[2,7,128,128]{3,2,1,0:T(8,128)S(1)} copy-done((f32[2,7,128,128]{3,2,1,0:T(8,128)S(1)}, f32[2,7,128,128]{3,2,1,0:T(8,128)}, u32[]{:S(2)}) %copy-start) | copy-done | bytes 917528
  1.9 0.0 copy-start.1
  1.9 1.0 %copy-done.1 = f32[1,8,128,128]{3,2,1,0:T(8,128)S(1)} copy-done((f32[1,8,128,128]{3,2,1,0:T(8,128)S(1)}, f32[1,8,128,128]{3,2,1,0:T(8,128)}, u32[]{:S(2)}) %copy-start.1) | copy-done | bytes 524312
  2.9 0.0 copy-start.2
  2.9 0.9 %copy-done.2 = f32[256,256]{1,0:T(8,128)S(1)} copy-done((f32[256,256]{1,0:T(8,128)S(1)}, f32[256,256]{1,0:T(8,128)}, u32[]{:S(2)}) %copy-start.2) | copy-done | bytes 262168
  3.9 0.0 copy-start.4
  3.9 0.7 %copy-done.4 = s32[2,7]{1,0:T(2,128)S(1)} copy-done((s32[2,7]{1,0:T(2,128)S(1)}, s32[2,7]{1,0:T(2,128)}, u32[]{:S(2)}) %copy-start.4) | copy-done | bytes 80
  4.5 0.0 copy-start.6
  4.5 0.7 %copy-done.6 = s32[1,8]{1,0:T(1,128)S(1)} copy-done((s32[1,8]{1,0:T(1,128)S(1)}, s32[1,8]{1,0:T(1,128)}, u32[]{:S(2)}) %copy-start.6) | copy-done | bytes 56
  5.2 38.1 %shard_map.73 = f32[256,256]{1,0:T(8,128)S(1)} custom-call(f32[256,256]{1,0:T(8,128)S(1)} %copy-done.2, f32[1,256]{1,0:T(1,128)S(1)} %bitcast.1, f32[2,7,128,128]{3,2,1,0:T(8,128)S(1)} %copy-done, s32[2,7]{1,0:T(2,128)S(1)} %copy-done.4, f32[1,8,128,128]{3,2,1,0:T(8,128)S(1)} %copy-done.1, s32[1,8]{1,0:T(1,128)S(1)} %copy-done.5, s32[1,8]{1,0:T(1,128)S(1)} %copy-done.6), custom_call_target="tpu_custom_call" | custom-call | tf_op jit(solution)/shard_map/pallas_call | solution.py:297
  43.3 0.7 %copy.9 = f32[256,256]{1,0:T(8,128)} copy(f32[256,256]{1,0:T(8,128)S(1)} %shard_map.73) | data formatting | bytes 524288
Async XLA Ops:
  0.0 0.7 %copy-start.5 = (s32[1,8]{1,0:T(1,128)S(1)}, s32[1,8]{1,0:T(1,128)}, u32[]{:S(2)}) copy-start(s32[1,8]{1,0:T(1,128)} %send_hbm.1) | copy-start | bytes 100
  0.0 0.7 %copy-start.3 = (f32[256]{0:T(256)S(1)}, f32[256]{0:T(256)}, u32[]{:S(2)}) copy-start(f32[256]{0:T(256)} %param.8) | copy-start | bytes 3076
  0.7 1.2 %copy-start = (f32[2,7,128,128]{3,2,1,0:T(8,128)S(1)}, f32[2,7,128,128]{3,2,1,0:T(8,128)}, u32[]{:S(2)}) copy-start(f32[2,7,128,128]{3,2,1,0:T(8,128)} %local.1) | copy-start | bytes 2752516
  1.9 1.0 %copy-start.1 = (f32[1,8,128,128]{3,2,1,0:T(8,128)S(1)}, f32[1,8,128,128]{3,2,1,0:T(8,128)}, u32[]{:S(2)}) copy-start(f32[1,8,128,128]{3,2,1,0:T(8,128)} %border.1) | copy-start | bytes 1572868
  2.9 0.9 %copy-start.2 = (f32[256,256]{1,0:T(8,128)S(1)}, f32[256,256]{1,0:T(8,128)}, u32[]{:S(2)}) copy-start(f32[256,256]{1,0:T(8,128)} %rhs.1) | copy-start | bytes 786436
  3.9 0.7 %copy-start.4 = (s32[2,7]{1,0:T(2,128)S(1)}, s32[2,7]{1,0:T(2,128)}, u32[]{:S(2)}) copy-start(s32[2,7]{1,0:T(2,128)} %cols_hbm.1) | copy-start | bytes 172
  4.5 0.7 %copy-start.6 = (s32[1,8]{1,0:T(1,128)S(1)}, s32[1,8]{1,0:T(1,128)}, u32[]{:S(2)}) copy-start(s32[1,8]{1,0:T(1,128)} %rows_hbm.1) | copy-start | bytes 100

commit v3 on v2

--- a/solution.py
+++ b/solution.py
@@ -7,13 +7,23 @@
 from jax.experimental.pallas import tpu as pltpu
 from jax.sharding import PartitionSpec as P
 
-HP = lax.Precision.HIGHEST
 LEFT, RIGHT, DOWN, UP = range(4)
 CHUNK = 128
 
 
+def halves(a):
+    high = a.astype(jnp.bfloat16)
+    return high, (a - high.astype(jnp.float32)).astype(jnp.bfloat16)
+
+
+def dot(a, b):
+    return jnp.dot(a, b, preferred_element_type=jnp.float32)
+
+
 def mm(a, b):
-    return jnp.dot(a, b, precision=HP, preferred_element_type=jnp.float32)
+    a_high, a_low = halves(a)
+    b_high, b_low = halves(b)
+    return dot(a_high, b_high) + (dot(a_high, b_low) + dot(a_low, b_high))
 
 
 def column_sum(a):
@@ -25,7 +35,7 @@
     rhs, diag_hbm, local, cols_hbm, border, send_hbm, rows_hbm,
     out,
     fields, images, prods_out, prods_in, local_v, border_v, border_in, pair_out, pair_in,
-    marks, marks_in, prec, work, sums, diag, cols, send, rows,
+    marks, marks_in, prec, turned, work, sums, diag, cols, send, rows,
     load_sem, f_send, f_recv, m_send, m_recv, k_send, k_recv, p_send, p_recv,
     b_send, b_recv, w_send, w_recv, s_send, s_recv,
 ):
@@ -94,12 +104,6 @@
             barrier, inc=1, device_id=peer(step), device_id_type=pl.DeviceIdType.MESH
         )
     )
-    loads[0].wait()
-    loads[1].wait()
-    for m in range(4 * per):
-        marks[m : m + 1, :] = jnp.full((1, 128), send[0, m], jnp.int32).astype(jnp.float32)
-        at = 4 * per + m
-        marks[at : at + 1, :] = jnp.full((1, 128), rows[0, m], jnp.int32).astype(jnp.float32)
     pl.semaphore_wait(barrier, total - 1)
 
     mark_copy = [
@@ -146,13 +150,16 @@
     pair = remote(pair_out, pair_in, p_send, p_recv, partner)
 
     for a in range(2):
+        given(has_next[a], lambda: border_copy[a].start())
+    field_pair.start()
+    loads[0].wait()
+    loads[1].wait()
+    for m in range(4 * per):
+        marks[m : m + 1, :] = jnp.full((1, 128), send[0, m], jnp.int32).astype(jnp.float32)
+        at = 4 * per + m
+        marks[at : at + 1, :] = jnp.full((1, 128), rows[0, m], jnp.int32).astype(jnp.float32)
+    for a in range(2):
         given(has_next[a], lambda: mark_copy[a].start())
-    for a in range(2):
-        given(has_next[a], lambda: border_copy[a].start())
-    for c in range(chunks):
-        for a in range(2):
-            given(has_next[a], lambda: field_copy[a][c].start())
-    field_pair.start()
 
     loads[2].wait()
     loads[3].wait()
@@ -168,36 +175,59 @@
             prec[0, i * bs : (i + 1) * bs, j * bs : (j + 1) * bs] = own
             pair_out[i * bs : (i + 1) * bs, j * bs : (j + 1) * bs] = far
     pair.start()
+    loads[4].wait()
+    for m in range(4 * per):
+        if m // per in came:
+            turned[m] = border_v[m].T
+    for a in range(2):
+        given(has_next[a], lambda: border_copy[a].wait_send())
+        given(has_next[a], lambda: field_copy[a][0].start())
     prec[0] = prec[0] + prec[0].T
-
-    loads[4].wait()
     loads[5].wait()
+
+    def weights(a, i, j):
+        turn, opp = came[a], goes[a]
+        for s in range(per):
+            m, n = turn * per + s, opp * per + s
+            at = 4 * per + n
+            yield (
+                jnp.where(rows[0, m] == i, 1.0, 0.0)
+                * jnp.where(marks_in[a, m : m + 1, :] == float(j), 1.0, 0.0),
+                jnp.where(send[0, n] == i, 1.0, 0.0)
+                * jnp.where(marks_in[a, at : at + 1, :] == float(j), 1.0, 0.0),
+                m,
+                s,
+            )
 
     def couple(a):
         mark_copy[a].wait_recv()
         border_copy[a].wait_recv()
-        turn, opp = came[a], goes[a]
-        back = [border_in[a, s].T for s in range(per)]
         for i in range(nb):
             for j in range(nb):
                 block = jnp.zeros((bs, bs), jnp.float32)
-                for s in range(per):
-                    m, n = turn * per + s, opp * per + s
-                    to = jnp.where(rows[0, m] == i, 1.0, 0.0)
-                    took = jnp.where(marks_in[a, m : m + 1, :] == float(j), 1.0, 0.0)
-                    block = block + (to * took) * border_v[m]
-                    to = jnp.where(send[0, n] == i, 1.0, 0.0)
-                    at = 4 * per + n
-                    took = jnp.where(marks_in[a, at : at + 1, :] == float(j), 1.0, 0.0)
-                    block = block + (to * took) * back[s]
-                prec[2 + a, i * bs : (i + 1) * bs, j * bs : (j + 1) * bs] = block
-        prec[4 + a] = prec[2 + a].T
-        for c in range(chunks):
+                for own, back, m, s in weights(a, i, j):
+                    block = block + own * turned[m] + back * border_in[a, s]
+                prec[4 + a, j * bs : (j + 1) * bs, i * bs : (i + 1) * bs] = block
+        prods_out[a, :, span(0)] = mm(prec[4 + a], fields[0, :, span(0)])
+        back_copy[a][0].start()
+
+    def finish(a):
+        for c in range(1, chunks):
             prods_out[a, :, span(c)] = mm(prec[4 + a], fields[0, :, span(c)])
             back_copy[a][c].start()
 
+    def uncouple(a):
+        prec[2 + a] = prec[4 + a].T
+
+    given(has_last[0], lambda: couple(0))
     given(has_last[1], lambda: couple(1))
-    given(has_last[0], lambda: couple(0))
+    for c in range(1, chunks):
+        for a in range(2):
+            given(has_next[a], lambda: field_copy[a][c].start())
+    given(has_last[0], lambda: finish(0))
+    given(has_last[1], lambda: finish(1))
+    given(has_last[0], lambda: uncouple(0))
+    given(has_last[1], lambda: uncouple(1))
 
     loads[6].wait()
     eye = lax.broadcasted_iota(jnp.int32, (size, size), 0) == lax.broadcasted_iota(
@@ -270,7 +300,6 @@
 
     for a in range(2):
         given(has_next[a], lambda: mark_copy[a].wait_send())
-        given(has_next[a], lambda: border_copy[a].wait_send())
         for c in range(chunks):
             given(has_next[a], lambda: field_copy[a][c].wait_send())
             given(has_last[a], lambda: back_copy[a][c].wait_send())
@@ -312,6 +341,7 @@
             pltpu.VMEM((2 * slots, 128), f32),
             pltpu.VMEM((2, 2 * slots, 128), f32),
             pltpu.VMEM((6, size, size), f32),
+            pltpu.VMEM((slots, bs, bs), f32),
             pltpu.VMEM((size, width), f32),
             pltpu.VMEM((2, total, 2, width), f32),
             pltpu.VMEM((1, size), f32),
@@ -323,7 +353,7 @@
             dma((2,)), dma((2,)),
         ],
         compiler_params=pltpu.CompilerParams(
-            collective_id=0, has_side_effects=True, vmem_limit_bytes=48 * 1024 * 1024
+            collective_id=0, has_side_effects=True
         ),
     )(
         right_side, node_diag.reshape(1, size), local_coup, block_cols, border_coup,

time: 44.3 us -> 39.2 us (0.88)
  local copies, waits for them, and re-layouts: 5.9 us -> 1.67 us
  Pallas kernels: 38.1 us -> 37.3 us
    unnamed x15 -> x1, local copies, waits for them, and re-layouts: 5.9 us -> 1.67 us
    pallas_call x1, Pallas kernels: 38.1 us -> 37.3 us  [shards(): pl.pallas_call(functools.partial(kernel, sizes), out_shape=jax.ShapeDtype...]
where the time goes in v3:
time: 39.2 us; the launch traced here: 39 us
  Pallas kernels  37.3 us (95%)
  local copies, waits for them, and re-layouts  1.67 us (4%)
    pallas_call x1, Pallas kernels, shards(): pl.pallas_call(functools.partial(kernel, sizes), out_shape=jax.ShapeDtype...  37.3 us
    unnamed x1, local copies, waits for them, and re-layouts  1.67 us

profile of v3, /device:TPU:0, one launch (start us, length us, event | category | flops | bytes accessed | tf_op | source)
XLA Modules:
  0.0 39.0 jit_solution(8313671022564379327)
XLA Ops:
  0.0 37.3 %shard_map.73 = f32[256,256]{1,0:T(8,128)} custom-call(f32[256,256]{1,0:T(8,128)} %rhs.1, f32[1,256]{1,0:T(1,128)} %bitcast.1, f32[2,7,128,128]{3,2,1,0:T(8,128)} %local.1, s32[2,7]{1,0:T(2,128)} %cols_hbm.1, f32[1,8,128,128]{3,2,1,0:T(8,128)} %border.1, s32[1,8]{1,0:T(1,128)} %send_hbm.1, s32[1,8]{1,0:T(1,128)} %rows_hbm.1), custom_call_target="tpu_custom_call" | custom-call | tf_op jit(solution)/shard_map/pallas_call | solution.py:326
  37.3 1.7 %copy.9 = f32[256,256]{1,0:T(8,128)} copy(f32[256,256]{1,0:T(8,128)} %shard_map.73) | data formatting | bytes 524288

commit v4 on v3

--- a/solution.py
+++ b/solution.py
@@ -33,9 +33,9 @@
 def kernel(
     sizes,
     rhs, diag_hbm, local, cols_hbm, border, send_hbm, rows_hbm,
-    out,
+    left_over, scale, scale_left,
     fields, images, prods_out, prods_in, local_v, border_v, border_in, pair_out, pair_in,
-    marks, marks_in, prec, turned, work, sums, diag, cols, send, rows,
+    marks, marks_in, prec, turned, work, residual, sums, diag, cols, send, rows,
     load_sem, f_send, f_recv, m_send, m_recv, k_send, k_recv, p_send, p_recv,
     b_send, b_recv, w_send, w_recv, s_send, s_recv,
 ):
@@ -43,7 +43,7 @@
     total = nx * ny * nn
     nb, nnz, bs, _ = local_v.shape
     per = border_v.shape[0] // 4
-    size, width = out.shape
+    size, width = left_over.shape
     chunks = width // CHUNK
     gx, gy, nd = lax.axis_index("gx"), lax.axis_index("gy"), lax.axis_index("nd")
     me = (gx * ny + gy) * nn + nd
@@ -79,10 +79,16 @@
 
     def over_peers(body):
         if total <= 16:
-            for step in range(1, total):
-                body(step)
+            xs = [lax.rem(gx + k, nx) for k in range(nx)]
+            ys = [lax.rem(gy + k, ny) for k in range(ny)]
+            ns = [lax.rem(nd + k, nn) for k in range(nn)]
+            for i in range(nx):
+                for j in range(ny):
+                    for k in range(nn):
+                        if (i, j, k) != (0, 0, 0):
+                            body({"gx": xs[i], "gy": ys[j], "nd": ns[k]})
         else:
-            lax.fori_loop(1, total, lambda step, _: (body(step), 0)[1], 0)
+            lax.fori_loop(1, total, lambda step, _: (body(peer(step)), 0)[1], 0)
 
     def remote(src, dst, ssem, rsem, where):
         return pltpu.make_async_remote_copy(
@@ -100,8 +106,8 @@
 
     barrier = pltpu.get_barrier_semaphore()
     over_peers(
-        lambda step: pl.semaphore_signal(
-            barrier, inc=1, device_id=peer(step), device_id_type=pl.DeviceIdType.MESH
+        lambda other: pl.semaphore_signal(
+            barrier, inc=1, device_id=other, device_id_type=pl.DeviceIdType.MESH
         )
     )
     pl.semaphore_wait(barrier, total - 1)
@@ -151,6 +157,8 @@
 
     for a in range(2):
         given(has_next[a], lambda: border_copy[a].start())
+    for a in range(2):
+        given(has_next[a], lambda: field_copy[a][0].start())
     field_pair.start()
     loads[0].wait()
     loads[1].wait()
@@ -179,9 +187,6 @@
     for m in range(4 * per):
         if m // per in came:
             turned[m] = border_v[m].T
-    for a in range(2):
-        given(has_next[a], lambda: border_copy[a].wait_send())
-        given(has_next[a], lambda: field_copy[a][0].start())
     prec[0] = prec[0] + prec[0].T
     loads[5].wait()
 
@@ -214,6 +219,7 @@
     def finish(a):
         for c in range(1, chunks):
             prods_out[a, :, span(c)] = mm(prec[4 + a], fields[0, :, span(c)])
+            back_copy[a][c - 1].wait_send()
             back_copy[a][c].start()
 
     def uncouple(a):
@@ -224,8 +230,6 @@
     for c in range(1, chunks):
         for a in range(2):
             given(has_next[a], lambda: field_copy[a][c].start())
-    given(has_last[0], lambda: finish(0))
-    given(has_last[1], lambda: finish(1))
     given(has_last[0], lambda: uncouple(0))
     given(has_last[1], lambda: uncouple(1))
 
@@ -241,6 +245,8 @@
     prec[1] = pair_out[...] + pair_in[...].T
     field_pair.wait()
     work[...] += mm(prec[1], fields[1])
+    given(has_last[1], lambda: finish(1))
+    given(has_last[0], lambda: finish(0))
 
     for c in range(chunks):
 
@@ -264,9 +270,9 @@
         sums[phase, me, 0:1, :] = first
         sums[phase, me, 1:2, :] = second
         over_peers(
-            lambda step: remote(
+            lambda other: remote(
                 sums.at[phase, me], sums.at[phase, me], s_send.at[phase], s_recv.at[phase],
-                peer(step),
+                other,
             ).start()
         )
 
@@ -282,8 +288,10 @@
     norm, curve = collect(0)
     alpha = norm / curve
 
-    out[...] = fields[0] - alpha * images[0]
-    work[...] = column * out[...] + mm(prec[0], out[...])
+    residual[...] = fields[0] - alpha * images[0]
+    store = pltpu.make_async_copy(residual, left_over, load_sem.at[0])
+    store.start()
+    work[...] = column * residual[...] + mm(prec[0], residual[...])
     for c in range(chunks):
 
         def quad_last(a):
@@ -296,13 +304,14 @@
         work[:, span(c)] += mm(prec[1], across)
         for a in (1, 0):
             given(has_last[a], lambda: quad_last(a))
-    share(1, column_sum(out[...] * out[...]), column_sum(out[...] * work[...]))
+    share(1, column_sum(residual[...] * residual[...]), column_sum(residual[...] * work[...]))
 
     for a in range(2):
         given(has_next[a], lambda: mark_copy[a].wait_send())
+        given(has_next[a], lambda: border_copy[a].wait_send())
+        given(has_last[a], lambda: back_copy[a][chunks - 1].wait_send())
         for c in range(chunks):
             given(has_next[a], lambda: field_copy[a][c].wait_send())
-            given(has_last[a], lambda: back_copy[a][c].wait_send())
             given(has_next[a], lambda: image_copy[a][c].wait_send())
     for c in range(chunks):
         image_copy[2][c].wait_send()
@@ -310,7 +319,9 @@
     norm_next, quad = collect(1)
     ratio = norm_next / norm
     alpha_next = norm_next / (quad - ratio * norm_next / alpha)
-    out[...] = (alpha + alpha_next * ratio) * fields[0] + alpha_next * out[...]
+    scale[...] = alpha + alpha_next * ratio
+    scale_left[...] = alpha_next
+    store.wait()
 
 
 def shards(sizes, right_side, node_diag, local_coup, block_cols, border_coup, border_send, border_rows):
@@ -323,11 +334,15 @@
     hbm = pl.BlockSpec(memory_space=pltpu.HBM)
     f32 = jnp.float32
     dma = pltpu.SemaphoreType.DMA
-    return pl.pallas_call(
+    left_over, scale, scale_left = pl.pallas_call(
         functools.partial(kernel, sizes),
-        out_shape=jax.ShapeDtypeStruct((size, width), f32),
+        out_shape=(
+            jax.ShapeDtypeStruct((size, width), f32),
+            jax.ShapeDtypeStruct((1, width), f32),
+            jax.ShapeDtypeStruct((1, width), f32),
+        ),
         in_specs=[hbm] * 7,
-        out_specs=pl.BlockSpec(memory_space=pltpu.VMEM),
+        out_specs=(hbm,) + (pl.BlockSpec(memory_space=pltpu.VMEM),) * 2,
         scratch_shapes=[
             pltpu.VMEM((4, size, width), f32),
             pltpu.VMEM((4, size, width), f32),
@@ -342,6 +357,7 @@
             pltpu.VMEM((2, 2 * slots, 128), f32),
             pltpu.VMEM((6, size, size), f32),
             pltpu.VMEM((slots, bs, bs), f32),
+            pltpu.VMEM((size, width), f32),
             pltpu.VMEM((size, width), f32),
             pltpu.VMEM((2, total, 2, width), f32),
             pltpu.VMEM((1, size), f32),
@@ -359,6 +375,7 @@
         right_side, node_diag.reshape(1, size), local_coup, block_cols, border_coup,
         border_send, border_rows,
     )
+    return scale * right_side + scale_left * left_over
 
 
 def solution(mesh):

time: 39.2 us -> 41.2 us (1.051)
  other arithmetic: 0 us -> 1.69 us
  Pallas kernels: 37.3 us -> 38.7 us
  local copies, waits for them, and re-layouts: 1.67 us -> 0.66 us
    add x0 -> x1, other arithmetic: none -> 1.69 us  [shards(): return scale * right_side + scale_left * left_over]
    pallas_call x1, Pallas kernels: 37.3 us -> 38.7 us  [shards(): pl.pallas_call(functools.partial(kernel, sizes), out_shape=(jax.ShapeDtyp...]
    unnamed x1 -> x6, local copies, waits for them, and re-layouts: 1.67 us -> 0.66 us
where the time goes in v4:
time: 41.2 us; the launch traced here: 41 us
  Pallas kernels  38.7 us (94%)
  other arithmetic  1.69 us (4%)
  local copies, waits for them, and re-layouts  0.66 us (2%)
    pallas_call x1, Pallas kernels, shards(): pl.pallas_call(functools.partial(kernel, sizes), out_shape=(jax.ShapeDtyp...  38.7 us
    add x1, other arithmetic, shards(): return scale * right_side + scale_left * left_over  1.69 us

profile of v4, /device:TPU:0, one launch (start us, length us, event | category | flops | bytes accessed | tf_op | source)
XLA Modules:
  0.0 41.0 jit_solution(14839192215701243300)
XLA Ops:
  0.0 0.0 copy-start
  0.0 38.7 %shard_map.73 = (f32[256,256]{1,0:T(8,128)}, f32[1,256]{1,0:T(1,128)}, f32[1,256]{1,0:T(1,128)}) custom-call(f32[256,256]{1,0:T(8,128)} %rhs.1, f32[1,256]{1,0:T(1,128)} %bitcast.3, f32[2,7,128,128]{3,2,1,0:T(8,128)} %local.1, s32[2,7]{1,0:T(2,128)} %cols_hbm.1, f32[1,8,128,128]{3,2,1,0:T(8,128)} %border.1, s32[1,8]{1,0:T(1,128)} %send_hbm.1, s32[1,8]{1,0:T(1,128)} %rows_hbm.1), custom_call_target="tpu_custom_call" | custom-call | tf_op jit(solution)/shard_map/pallas_call | solution.py:337
  38.7 0.0 copy-start.2
  38.7 0.0 copy-start.1
  38.7 0.0 copy-done
  38.7 0.7 %copy-done.2 = f32[1,256]{1,0:T(1,128)S(1)} copy-done((f32[1,256]{1,0:T(1,128)S(1)}, f32[1,256]{1,0:T(1,128)}, u32[]{:S(2)}) %copy-start.2) | copy-done | bytes 1048
  39.3 0.0 copy-done.1
  39.4 1.7 %multiply_add_fusion = f32[256,256]{1,0:T(8,128)} fusion(f32[256,256]{1,0:T(8,128)} %get-tuple-element.10, f32[256,256]{1,0:T(8,128)S(1)} %copy-done, f32[256]{0:T(256)S(1)} %bitcast.5, f32[256]{0:T(256)S(1)} %bitcast.4), kind=kLoop, calls=%fused_computation | loop fusion | flops 196608 | bytes 788480 | tf_op jit(solution)/shard_map/add | solution.py:378
Async XLA Ops:
  0.0 38.7 %copy-start = (f32[256,256]{1,0:T(8,128)S(1)}, f32[256,256]{1,0:T(8,128)}, u32[]{:S(2)}) copy-start(f32[256,256]{1,0:T(8,128)} %rhs.1) | copy-start | bytes 786436
  38.7 0.7 %copy-start.2 = (f32[1,256]{1,0:T(1,128)S(1)}, f32[1,256]{1,0:T(1,128)}, u32[]{:S(2)}) copy-start(f32[1,256]{1,0:T(1,128)} %get-tuple-element.9) | copy-start | bytes 3076
  38.7 0.7 %copy-start.1 = (f32[1,256]{1,0:T(1,128)S(1)}, f32[1,256]{1,0:T(1,128)}, u32[]{:S(2)}) copy-start(f32[1,256]{1,0:T(1,128)} %get-tuple-element.8) | copy-start | bytes 3076

commit v5 on v3

--- a/solution.py
+++ b/solution.py
@@ -79,10 +79,16 @@
 
     def over_peers(body):
         if total <= 16:
-            for step in range(1, total):
-                body(step)
+            xs = [lax.rem(gx + k, nx) for k in range(nx)]
+            ys = [lax.rem(gy + k, ny) for k in range(ny)]
+            ns = [lax.rem(nd + k, nn) for k in range(nn)]
+            for i in range(nx):
+                for j in range(ny):
+                    for k in range(nn):
+                        if (i, j, k) != (0, 0, 0):
+                            body({"gx": xs[i], "gy": ys[j], "nd": ns[k]})
         else:
-            lax.fori_loop(1, total, lambda step, _: (body(step), 0)[1], 0)
+            lax.fori_loop(1, total, lambda step, _: (body(peer(step)), 0)[1], 0)
 
     def remote(src, dst, ssem, rsem, where):
         return pltpu.make_async_remote_copy(
@@ -100,8 +106,8 @@
 
     barrier = pltpu.get_barrier_semaphore()
     over_peers(
-        lambda step: pl.semaphore_signal(
-            barrier, inc=1, device_id=peer(step), device_id_type=pl.DeviceIdType.MESH
+        lambda other: pl.semaphore_signal(
+            barrier, inc=1, device_id=other, device_id_type=pl.DeviceIdType.MESH
         )
     )
     pl.semaphore_wait(barrier, total - 1)
@@ -185,6 +191,14 @@
     prec[0] = prec[0] + prec[0].T
     loads[5].wait()
 
+    loads[6].wait()
+    eye = lax.broadcasted_iota(jnp.int32, (size, size), 0) == lax.broadcasted_iota(
+        jnp.int32, (size, size), 1
+    )
+    column = jnp.sum(
+        jnp.where(eye, jnp.broadcast_to(diag[...], (size, size)), 0.0), axis=1, keepdims=True
+    )
+    work[...] = column * fields[0] + mm(prec[0], fields[0])
     def weights(a, i, j):
         turn, opp = came[a], goes[a]
         for s in range(per):
@@ -211,36 +225,26 @@
         prods_out[a, :, span(0)] = mm(prec[4 + a], fields[0, :, span(0)])
         back_copy[a][0].start()
 
-    def finish(a):
-        for c in range(1, chunks):
-            prods_out[a, :, span(c)] = mm(prec[4 + a], fields[0, :, span(c)])
-            back_copy[a][c].start()
+    def follow(a, c):
+        prods_out[a, :, span(c)] = mm(prec[4 + a], fields[0, :, span(c)])
+        back_copy[a][c - 1].wait_send()
+        back_copy[a][c].start()
 
     def uncouple(a):
         prec[2 + a] = prec[4 + a].T
 
     given(has_last[0], lambda: couple(0))
     given(has_last[1], lambda: couple(1))
-    for c in range(1, chunks):
-        for a in range(2):
-            given(has_next[a], lambda: field_copy[a][c].start())
-    given(has_last[0], lambda: finish(0))
-    given(has_last[1], lambda: finish(1))
-    given(has_last[0], lambda: uncouple(0))
-    given(has_last[1], lambda: uncouple(1))
-
-    loads[6].wait()
-    eye = lax.broadcasted_iota(jnp.int32, (size, size), 0) == lax.broadcasted_iota(
-        jnp.int32, (size, size), 1
-    )
-    column = jnp.sum(
-        jnp.where(eye, jnp.broadcast_to(diag[...], (size, size)), 0.0), axis=1, keepdims=True
-    )
-    work[...] = column * fields[0] + mm(prec[0], fields[0])
     pair.wait()
     prec[1] = pair_out[...] + pair_in[...].T
     field_pair.wait()
     work[...] += mm(prec[1], fields[1])
+    for c in range(1, chunks):
+        for a in range(2):
+            given(has_last[a], lambda: follow(a, c))
+            given(has_next[a], lambda: field_copy[a][c].start())
+    given(has_last[0], lambda: uncouple(0))
+    given(has_last[1], lambda: uncouple(1))
 
     for c in range(chunks):
 
@@ -264,9 +268,9 @@
         sums[phase, me, 0:1, :] = first
         sums[phase, me, 1:2, :] = second
         over_peers(
-            lambda step: remote(
+            lambda other: remote(
                 sums.at[phase, me], sums.at[phase, me], s_send.at[phase], s_recv.at[phase],
-                peer(step),
+                other,
             ).start()
         )
 
@@ -300,9 +304,9 @@
 
     for a in range(2):
         given(has_next[a], lambda: mark_copy[a].wait_send())
+        given(has_last[a], lambda: back_copy[a][chunks - 1].wait_send())
         for c in range(chunks):
             given(has_next[a], lambda: field_copy[a][c].wait_send())
-            given(has_last[a], lambda: back_copy[a][c].wait_send())
             given(has_next[a], lambda: image_copy[a][c].wait_send())
     for c in range(chunks):
         image_copy[2][c].wait_send()

time: 39.2 us -> 39.4 us (level)
  no operation moved by 1% of the time
where the time goes in v5:
time: 39.4 us; the launch traced here: 39.3 us
  Pallas kernels  37.6 us (95%)
  local copies, waits for them, and re-layouts  1.67 us (4%)
    pallas_call x1, Pallas kernels, shards(): pl.pallas_call(functools.partial(kernel, sizes), out_shape=jax.ShapeDtype...  37.6 us
    unnamed x1, local copies, waits for them, and re-layouts  1.67 us

profile of v5, /device:TPU:0, one launch (start us, length us, event | category | flops | bytes accessed | tf_op | source)
XLA Modules:
  0.0 39.3 jit_solution(11278230042455097647)
XLA Ops:
  0.0 37.6 %shard_map.73 = f32[256,256]{1,0:T(8,128)} custom-call(f32[256,256]{1,0:T(8,128)} %rhs.1, f32[1,256]{1,0:T(1,128)} %bitcast.1, f32[2,7,128,128]{3,2,1,0:T(8,128)} %local.1, s32[2,7]{1,0:T(2,128)} %cols_hbm.1, f32[1,8,128,128]{3,2,1,0:T(8,128)} %border.1, s32[1,8]{1,0:T(1,128)} %send_hbm.1, s32[1,8]{1,0:T(1,128)} %rows_hbm.1), custom_call_target="tpu_custom_call" | custom-call | tf_op jit(solution)/shard_map/pallas_call | solution.py:330
  37.6 1.7 %copy.9 = f32[256,256]{1,0:T(8,128)} copy(f32[256,256]{1,0:T(8,128)} %shard_map.73) | data formatting | bytes 524288

commit v6 on v5

--- a/solution.py
+++ b/solution.py
@@ -35,7 +35,7 @@
     rhs, diag_hbm, local, cols_hbm, border, send_hbm, rows_hbm,
     out,
     fields, images, prods_out, prods_in, local_v, border_v, border_in, pair_out, pair_in,
-    marks, marks_in, prec, turned, work, sums, diag, cols, send, rows,
+    marks, marks_in, prec, turned, work, half, sums, diag, cols, send, rows,
     load_sem, f_send, f_recv, m_send, m_recv, k_send, k_recv, p_send, p_recv,
     b_send, b_recv, w_send, w_recv, s_send, s_recv,
 ):
@@ -198,7 +198,8 @@
     column = jnp.sum(
         jnp.where(eye, jnp.broadcast_to(diag[...], (size, size)), 0.0), axis=1, keepdims=True
     )
-    work[...] = column * fields[0] + mm(prec[0], fields[0])
+    half[...] = mm(prec[0], fields[0])
+
     def weights(a, i, j):
         turn, opp = came[a], goes[a]
         for s in range(per):
@@ -238,7 +239,8 @@
     pair.wait()
     prec[1] = pair_out[...] + pair_in[...].T
     field_pair.wait()
-    work[...] += mm(prec[1], fields[1])
+    half[...] += mm(prec[1], fields[1])
+    work[...] = column * fields[0] + half[...]
     for c in range(1, chunks):
         for a in range(2):
             given(has_last[a], lambda: follow(a, c))
@@ -250,7 +252,9 @@
 
         def from_last(a):
             field_copy[a][c].wait_recv()
-            work[:, span(c)] += mm(prec[2 + a], fields[2 + a, :, span(c)])
+            term = mm(prec[2 + a], fields[2 + a, :, span(c)])
+            work[:, span(c)] += term
+            half[:, span(c)] += 2.0 * term
 
         def from_next(a):
             back_copy[a][c].wait_recv()
@@ -283,23 +287,23 @@
         return both[0:1, :], both[1:2, :]
 
     share(0, column_sum(fields[0] * fields[0]), column_sum(fields[0] * images[0]))
+
+    work[...] = mm(prec[0], images[0])
+    for c in range(chunks):
+
+        def quad_last(a):
+            image_copy[a][c].wait_recv()
+            work[:, span(c)] += 2.0 * mm(prec[2 + a], images[2 + a, :, span(c)])
+
+        image_copy[2][c].wait_recv()
+        work[:, span(c)] += mm(prec[1], images[1, :, span(c)])
+        for a in (1, 0):
+            given(has_last[a], lambda: quad_last(a))
+
     norm, curve = collect(0)
     alpha = norm / curve
-
     out[...] = fields[0] - alpha * images[0]
-    work[...] = column * out[...] + mm(prec[0], out[...])
-    for c in range(chunks):
-
-        def quad_last(a):
-            image_copy[a][c].wait_recv()
-            behind = fields[2 + a, :, span(c)] - alpha[:, span(c)] * images[2 + a, :, span(c)]
-            work[:, span(c)] += 2.0 * mm(prec[2 + a], behind)
-
-        image_copy[2][c].wait_recv()
-        across = fields[1, :, span(c)] - alpha[:, span(c)] * images[1, :, span(c)]
-        work[:, span(c)] += mm(prec[1], across)
-        for a in (1, 0):
-            given(has_last[a], lambda: quad_last(a))
+    work[...] = column * out[...] + (half[...] - alpha * work[...])
     share(1, column_sum(out[...] * out[...]), column_sum(out[...] * work[...]))
 
     for a in range(2):
@@ -347,6 +351,7 @@
             pltpu.VMEM((6, size, size), f32),
             pltpu.VMEM((slots, bs, bs), f32),
             pltpu.VMEM((size, width), f32),
+            pltpu.VMEM((size, width), f32),
             pltpu.VMEM((2, total, 2, width), f32),
             pltpu.VMEM((1, size), f32),
             pltpu.SMEM((nb, nnz), jnp.int32),

time: 39.4 us -> 37.5 us (0.952)
  Pallas kernels: 37.6 us -> 35.7 us
    pallas_call x1, Pallas kernels: 37.6 us -> 35.7 us  [shards(): pl.pallas_call(functools.partial(kernel, sizes), out_shape=jax.ShapeDtype...]
where the time goes in v6:
time: 37.5 us; the launch traced here: 37.3 us
  Pallas kernels  35.7 us (95%)
  local copies, waits for them, and re-layouts  1.67 us (4%)
    pallas_call x1, Pallas kernels, shards(): pl.pallas_call(functools.partial(kernel, sizes), out_shape=jax.ShapeDtype...  35.7 us
    unnamed x1, local copies, waits for them, and re-layouts  1.67 us

profile of v6, /device:TPU:0, one launch (start us, length us, event | category | flops | bytes accessed | tf_op | source)
XLA Modules:
  0.0 37.3 jit_solution(16101837372975005855)
XLA Ops:
  0.0 35.7 %shard_map.73 = f32[256,256]{1,0:T(8,128)} custom-call(f32[256,256]{1,0:T(8,128)} %rhs.1, f32[1,256]{1,0:T(1,128)} %bitcast.1, f32[2,7,128,128]{3,2,1,0:T(8,128)} %local.1, s32[2,7]{1,0:T(2,128)} %cols_hbm.1, f32[1,8,128,128]{3,2,1,0:T(8,128)} %border.1, s32[1,8]{1,0:T(1,128)} %send_hbm.1, s32[1,8]{1,0:T(1,128)} %rows_hbm.1), custom_call_target="tpu_custom_call" | custom-call | tf_op jit(solution)/shard_map/pallas_call | solution.py:334
  35.7 1.7 %copy.9 = f32[256,256]{1,0:T(8,128)} copy(f32[256,256]{1,0:T(8,128)} %shard_map.73) | data formatting | bytes 524288

commit v7 on v6

--- a/solution.py
+++ b/solution.py
@@ -9,6 +9,7 @@
 
 LEFT, RIGHT, DOWN, UP = range(4)
 CHUNK = 128
+PIECES = 4
 
 
 def halves(a):
@@ -23,7 +24,23 @@
 def mm(a, b):
     a_high, a_low = halves(a)
     b_high, b_low = halves(b)
-    return dot(a_high, b_high) + (dot(a_high, b_low) + dot(a_low, b_high))
+    width = b.shape[1]
+    both = dot(a_high, jnp.concatenate([b_high, b_low], axis=1))
+    return both[:, :width] + (both[:, width:] + dot(a_low, b_high))
+
+
+def hand_over(found, out, sems):
+    rows = out.shape[0] // PIECES
+    copies = [
+        pltpu.make_async_copy(
+            found.at[pl.ds(i * rows, rows)], out.at[pl.ds(i * rows, rows)], sems.at[i]
+        )
+        for i in range(PIECES)
+    ]
+    for copy in copies:
+        copy.start()
+    for copy in copies:
+        copy.wait()
 
 
 def column_sum(a):
@@ -331,7 +348,7 @@
     hbm = pl.BlockSpec(memory_space=pltpu.HBM)
     f32 = jnp.float32
     dma = pltpu.SemaphoreType.DMA
-    return pl.pallas_call(
+    found = pl.pallas_call(
         functools.partial(kernel, sizes),
         out_shape=jax.ShapeDtypeStruct((size, width), f32),
         in_specs=[hbm] * 7,
@@ -368,6 +385,13 @@
         right_side, node_diag.reshape(1, size), local_coup, block_cols, border_coup,
         border_send, border_rows,
     )
+    return pl.pallas_call(
+        hand_over,
+        out_shape=jax.ShapeDtypeStruct((size, width), f32),
+        in_specs=[hbm],
+        out_specs=hbm,
+        scratch_shapes=[dma((PIECES,))],
+    )(found)
 
 
 def solution(mesh):

time: 37.5 us -> 44.9 us (1.20)
  Pallas kernels: 35.7 us -> 44.7 us
  local copies, waits for them, and re-layouts: 1.67 us -> 0 us
    pallas_call x0 -> x1, Pallas kernels: none -> 9.08 us  [shards(): pl.pallas_call(hand_over, out_shape=jax.ShapeDtypeStruct((size, width), f...]
    unnamed x1 -> x0, local copies, waits for them, and re-layouts: 1.67 us -> none
where the time goes in v7:
time: 44.9 us; the launch traced here: 44.7 us
  Pallas kernels  44.7 us (100%)
    pallas_call x1, Pallas kernels, shards(): pl.pallas_call(functools.partial(kernel, sizes), out_shape=jax.ShapeDtype...  35.7 us
    pallas_call x1, Pallas kernels, shards(): pl.pallas_call(hand_over, out_shape=jax.ShapeDtypeStruct((size, width), f...  9.08 us

profile of v7, /device:TPU:0, one launch (start us, length us, event | category | flops | bytes accessed | tf_op | source)
XLA Modules:
  0.0 44.7 jit_solution(8839099023403110957)
XLA Ops:
  0.0 35.7 %shard_map.73.found = f32[256,256]{1,0:T(8,128)} custom-call(f32[256,256]{1,0:T(8,128)} %rhs.1, f32[1,256]{1,0:T(1,128)} %bitcast.1, f32[2,7,128,128]{3,2,1,0:T(8,128)} %local.1, s32[2,7]{1,0:T(2,128)} %cols_hbm.1, f32[1,8,128,128]{3,2,1,0:T(8,128)} %border.1, s32[1,8]{1,0:T(1,128)} %send_hbm.1, s32[1,8]{1,0:T(1,128)} %rows_hbm.1), custom_call_target="tpu_custom_call" | custom-call | tf_op jit(solution)/shard_map/pallas_call | solution.py:351
  35.7 9.1 %shard_map.74 = f32[256,256]{1,0:T(8,128)} custom-call(f32[256,256]{1,0:T(8,128)} %shard_map.73.found), custom_call_target="tpu_custom_call" | custom-call | tf_op jit(solution)/shard_map/pallas_call | solution.py:388

commit v8 on v6

--- a/solution.py
+++ b/solution.py
@@ -23,7 +23,9 @@
 def mm(a, b):
     a_high, a_low = halves(a)
     b_high, b_low = halves(b)
-    return dot(a_high, b_high) + (dot(a_high, b_low) + dot(a_low, b_high))
+    width = b.shape[1]
+    both = dot(a_high, jnp.concatenate([b_high, b_low], axis=1))
+    return both[:, :width] + (both[:, width:] + dot(a_low, b_high))
 
 
 def column_sum(a):
@@ -101,8 +103,8 @@
         (border.at[0], border_v), (rhs, fields.at[0]), (diag_hbm, diag),
     )
     loads = [pltpu.make_async_copy(src, dst, load_sem.at[i]) for i, (src, dst) in enumerate(pairs)]
-    for load in loads:
-        load.start()
+    for i in (4, 5, 0, 1, 2, 3, 6):
+        loads[i].start()
 
     barrier = pltpu.get_barrier_semaphore()
     over_peers(
@@ -117,7 +119,7 @@
     ]
     border_copy = [
         remote(
-            border.at[0, pl.ds(goes[a] * per, per)], border_in.at[a],
+            border_v.at[pl.ds(goes[a] * per, per)], border_in.at[a],
             m_send.at[a], m_recv.at[a], forward[a],
         )
         for a in range(2)
@@ -125,7 +127,7 @@
     field_copy = [
         [
             remote(
-                rhs.at[:, part(c)], fields.at[2 + a, :, part(c)],
+                fields.at[0, :, part(c)], fields.at[2 + a, :, part(c)],
                 f_send.at[a, c], f_recv.at[a, c], forward[a],
             )
             for c in range(chunks)
@@ -152,11 +154,13 @@
         ]
         for i, (slot, where) in enumerate(((2, right), (3, above), (1, partner)))
     ]
-    field_pair = remote(rhs, fields.at[1], f_send.at[2, 0], f_recv.at[2, 0], partner)
+    field_pair = remote(fields.at[0], fields.at[1], f_send.at[2, 0], f_recv.at[2, 0], partner)
     pair = remote(pair_out, pair_in, p_send, p_recv, partner)
 
+    loads[4].wait()
     for a in range(2):
         given(has_next[a], lambda: border_copy[a].start())
+    loads[5].wait()
     field_pair.start()
     loads[0].wait()
     loads[1].wait()
@@ -181,7 +185,6 @@
             prec[0, i * bs : (i + 1) * bs, j * bs : (j + 1) * bs] = own
             pair_out[i * bs : (i + 1) * bs, j * bs : (j + 1) * bs] = far
     pair.start()
-    loads[4].wait()
     for m in range(4 * per):
         if m // per in came:
             turned[m] = border_v[m].T
@@ -189,7 +192,6 @@
         given(has_next[a], lambda: border_copy[a].wait_send())
         given(has_next[a], lambda: field_copy[a][0].start())
     prec[0] = prec[0] + prec[0].T
-    loads[5].wait()
 
     loads[6].wait()
     eye = lax.broadcasted_iota(jnp.int32, (size, size), 0) == lax.broadcasted_iota(

time: 37.5 us -> 37.1 us (0.989)
  Pallas kernels: 35.7 us -> 35.3 us
    pallas_call x1, Pallas kernels: 35.7 us -> 35.3 us  [shards(): pl.pallas_call(functools.partial(kernel, sizes), out_shape=jax.ShapeDtype...]
where the time goes in v8:
time: 37.1 us; the launch traced here: 37 us
  Pallas kernels  35.3 us (95%)
  local copies, waits for them, and re-layouts  1.67 us (5%)
    pallas_call x1, Pallas kernels, shards(): pl.pallas_call(functools.partial(kernel, sizes), out_shape=jax.ShapeDtype...  35.3 us
    unnamed x1, local copies, waits for them, and re-layouts  1.67 us

profile of v8, /device:TPU:0, one launch (start us, length us, event | category | flops | bytes accessed | tf_op | source)
XLA Modules:
  0.0 37.0 jit_solution(5062577108445989941)
XLA Ops:
  0.0 35.3 %shard_map.73 = f32[256,256]{1,0:T(8,128)} custom-call(f32[256,256]{1,0:T(8,128)} %rhs.1, f32[1,256]{1,0:T(1,128)} %bitcast.1, f32[2,7,128,128]{3,2,1,0:T(8,128)} %local.1, s32[2,7]{1,0:T(2,128)} %cols_hbm.1, f32[1,8,128,128]{3,2,1,0:T(8,128)} %border.1, s32[1,8]{1,0:T(1,128)} %send_hbm.1, s32[1,8]{1,0:T(1,128)} %rows_hbm.1), custom_call_target="tpu_custom_call" | custom-call | tf_op jit(solution)/shard_map/pallas_call | solution.py:336
  35.3 1.7 %copy.9 = f32[256,256]{1,0:T(8,128)} copy(f32[256,256]{1,0:T(8,128)} %shard_map.73) | data formatting | bytes 524288

commit v9 on v8

--- a/solution.py
+++ b/solution.py
@@ -250,26 +250,6 @@
     given(has_last[0], lambda: uncouple(0))
     given(has_last[1], lambda: uncouple(1))
 
-    for c in range(chunks):
-
-        def from_last(a):
-            field_copy[a][c].wait_recv()
-            term = mm(prec[2 + a], fields[2 + a, :, span(c)])
-            work[:, span(c)] += term
-            half[:, span(c)] += 2.0 * term
-
-        def from_next(a):
-            back_copy[a][c].wait_recv()
-            work[:, span(c)] += prods_in[a, :, span(c)]
-
-        for a in (1, 0):
-            given(has_last[a], lambda: from_last(a))
-            given(has_next[a], lambda: from_next(a))
-        images[0, :, span(c)] = work[:, span(c)]
-        image_copy[0][c].start()
-        given(high, lambda: image_copy[1][c].start())
-        image_copy[2][c].start()
-
     def share(phase, first, second):
         sums[phase, me, 0:1, :] = first
         sums[phase, me, 1:2, :] = second
@@ -280,6 +260,29 @@
             ).start()
         )
 
+    norm_here = column_sum(fields[0] * fields[0])
+    for c in range(chunks):
+
+        def from_last(a):
+            field_copy[a][c].wait_recv()
+            term = mm(prec[2 + a], fields[2 + a, :, span(c)])
+            work[:, span(c)] += term
+            half[:, span(c)] += 2.0 * term
+
+        def from_next(a):
+            back_copy[a][c].wait_recv()
+            work[:, span(c)] += prods_in[a, :, span(c)]
+
+        for a in (1, 0):
+            given(has_last[a], lambda: from_last(a))
+            given(has_next[a], lambda: from_next(a))
+        images[0, :, span(c)] = work[:, span(c)]
+        if c == chunks - 1:
+            share(0, norm_here, column_sum(fields[0] * images[0]))
+        image_copy[0][c].start()
+        given(high, lambda: image_copy[1][c].start())
+        image_copy[2][c].start()
+
     def collect(phase):
         every = sums.at[phase, pl.ds(0, total - 1)]
         done = remote(every, every, s_send.at[phase], s_recv.at[phase], partner)
@@ -288,7 +291,6 @@
         both = jnp.sum(sums[phase], axis=0)
         return both[0:1, :], both[1:2, :]
 
-    share(0, column_sum(fields[0] * fields[0]), column_sum(fields[0] * images[0]))
 
     work[...] = mm(prec[0], images[0])
     for c in range(chunks):

time: 37.1 us -> 36.3 us (0.978)
  Pallas kernels: 35.3 us -> 34.4 us
    pallas_call x1, Pallas kernels: 35.3 us -> 34.4 us  [shards(): pl.pallas_call(functools.partial(kernel, sizes), out_shape=jax.ShapeDtype...]
where the time goes in v9:
time: 36.3 us; the launch traced here: 36.1 us
  Pallas kernels  34.4 us (95%)
  local copies, waits for them, and re-layouts  1.67 us (5%)
    pallas_call x1, Pallas kernels, shards(): pl.pallas_call(functools.partial(kernel, sizes), out_shape=jax.ShapeDtype...  34.4 us
    unnamed x1, local copies, waits for them, and re-layouts  1.67 us

profile of v9, /device:TPU:0, one launch (start us, length us, event | category | flops | bytes accessed | tf_op | source)
XLA Modules:
  0.0 36.1 jit_solution(5345244653444191947)
XLA Ops:
  0.0 34.4 %shard_map.73 = f32[256,256]{1,0:T(8,128)} custom-call(f32[256,256]{1,0:T(8,128)} %rhs.1, f32[1,256]{1,0:T(1,128)} %bitcast.1, f32[2,7,128,128]{3,2,1,0:T(8,128)} %local.1, s32[2,7]{1,0:T(2,128)} %cols_hbm.1, f32[1,8,128,128]{3,2,1,0:T(8,128)} %border.1, s32[1,8]{1,0:T(1,128)} %send_hbm.1, s32[1,8]{1,0:T(1,128)} %rows_hbm.1), custom_call_target="tpu_custom_call" | custom-call | tf_op jit(solution)/shard_map/pallas_call | solution.py:338
  34.5 1.7 %copy.9 = f32[256,256]{1,0:T(8,128)} copy(f32[256,256]{1,0:T(8,128)} %shard_map.73) | data formatting | bytes 524288
